TPU v7x, 32 devices: a whole 2x2x4 slice. The times are simulated.
32 devices in a mesh: groups: 2 (over y), ep: 16 (over z, x, core).
Axes of the slice: x: 2, y: 2, z: 4, core: 2. Of those that a mesh axis runs over, the one named last changes fastest.
Arguments:
- tokens: bfloat16 [2048, 2880], P(('groups', 'ep')), parts along dimension 0, may hold values from -6 to 6
- expert_ids: int32 [2048, 4], P(('groups', 'ep')), parts along dimension 0, may hold values from 0 to 15, all different within a row; in each aligned block of 64 rows (0 to 63, 64 to 127, ...) at most 18 rows name the same one
- gate_ints: int32 [2048, 4], P(('groups', 'ep')), parts along dimension 0, may hold values from 1 to 255
- norm_gain: float32 [2880], replicated, may hold values from 0.5 to 2
- weight_in: bfloat16 [16, 2880, 5760], P('ep'), may hold values from -0.109375 to 0.109375
- bias_in: float32 [16, 5760], P('ep'), may hold values from -3 to 3
- weight_out: bfloat16 [16, 2880, 2880], P('ep'), may hold values from -0.109375 to 0.109375
- bias_out: float32 [16, 2880], replicated, may hold values from -3 to 3
Outputs:
- mixed: bfloat16 [2048, 2880], P(('groups', 'ep')), parts along dimension 0
There are 2 independent parts, one for each index of `groups`. A program takes and returns all parts, laid end to end along the dimension named above; an argument that names none is the same for every part. Nothing has to cross between parts.
Inputs may be any that keep to these rules, and one draw needn't show every extreme that they name: `expert_ids`: each row names 4 different experts. Within the rows of one device (aligned blocks of 64 rows) no expert is named more than 18 times.
All inputs are finite; a program needn't handle non-finite values.
Results may differ from a plain program's by a relative error of at most 0.0065.
Values may be sent and summed in bfloat16 or wider, within the bound.
No kernel may reach another device: no remote copies, remote signals or barrier semaphores. Data moves between devices by JAX's collectives and lax.ppermute only.
A program may use at most 256 MiB of HBM per device.

v0:
```python
import jax
import jax.numpy as jnp
from jax import lax
from jax.sharding import PartitionSpec as P

CAP = 18


def shards(tokens, expert_ids, gate_ints, norm_gain, weight_in, bias_in, weight_out, bias_out):
    device_count = lax.axis_size("ep")
    expert_count = bias_out.shape[0]
    part_count = device_count // expert_count
    row_count, model_width = tokens.shape
    top_count = expert_ids.shape[1]
    capacity = CAP
    tok_float = tokens.astype(jnp.float32)
    row_scale = lax.rsqrt(jnp.mean(tok_float * tok_float, axis=1, keepdims=True) + 1e-05)
    normed = (tok_float * row_scale * norm_gain[None, :]).astype(jnp.bfloat16)
    int_gates = gate_ints.astype(jnp.float32)
    route_weight = int_gates / jnp.sum(int_gates, axis=1, keepdims=True)
    flat_ids = expert_ids.reshape(row_count * top_count)
    one_hot = (flat_ids[:, None] == jnp.arange(expert_count, dtype=jnp.int32)[None, :]).astype(
        jnp.int32
    )
    slot_rank = jnp.sum((jnp.cumsum(one_hot, axis=0) - one_hot) * one_hot, axis=1)
    slot_target = (flat_ids * capacity + slot_rank).reshape(row_count, top_count)
    slot_ids = jnp.arange(expert_count * capacity, dtype=jnp.int32)
    slot_match = slot_target[None, :, :] == slot_ids[:, None, None]
    picker = jnp.any(slot_match, axis=2).astype(jnp.bfloat16)
    placed = jnp.dot(picker, normed, preferred_element_type=jnp.float32).astype(jnp.bfloat16)
    combiner = jnp.transpose(jnp.sum(jnp.where(slot_match, route_weight[None, :, :], 0.0), axis=2))
    outgoing = jnp.broadcast_to(
        placed.reshape(expert_count, 1, capacity, model_width),
        (expert_count, part_count, capacity, model_width),
    ).reshape(device_count, capacity, model_width)
    arrived = lax.all_to_all(outgoing, "ep", split_axis=0, concat_axis=0, tiled=True)
    source_count = arrived.shape[0]
    slot_count = arrived.shape[1]
    flat_rows = arrived.reshape(source_count * slot_count, model_width)
    pre_act = (
        jnp.dot(flat_rows, weight_in[0], preferred_element_type=jnp.float32) + bias_in[0][None, :]
    )
    half_width = pre_act.shape[1] // 2
    gate_part = pre_act[:, :half_width]
    up_part = pre_act[:, half_width:]
    activated = (gate_part * jax.nn.sigmoid(1.702 * gate_part) * (up_part + 1.0)).astype(
        jnp.bfloat16
    )
    result = jnp.dot(activated, weight_out[0], preferred_element_type=jnp.float32).astype(
        jnp.bfloat16
    )
    returned = lax.all_to_all(
        result.reshape(source_count, slot_count, model_width),
        "ep",
        split_axis=0,
        concat_axis=0,
        tiled=True,
    )
    part_sum = jnp.sum(
        returned.reshape(expert_count, part_count, capacity, model_width), axis=1, dtype=jnp.float32
    ).reshape(expert_count * capacity, model_width)
    moe_rows = jnp.dot(combiner, part_sum, precision=lax.Precision.HIGHEST)
    expert_hot = expert_ids[:, :, None] == jnp.arange(expert_count, dtype=jnp.int32)[None, None, :]
    expert_weight = jnp.sum(jnp.where(expert_hot, route_weight[:, :, None], 0.0), axis=1)
    bias_term = jnp.dot(expert_weight, bias_out, precision=lax.Precision.HIGHEST)
    return (tok_float + moe_rows + bias_term).astype(jnp.bfloat16)


def solution(mesh):
    return jax.shard_map(
        shards,
        mesh=mesh,
        in_specs=(
            P(("groups", "ep"), None),
            P(("groups", "ep"), None),
            P(("groups", "ep"), None),
            P(),
            P("ep", None, None),
            P("ep", None),
            P("ep", None, None),
            P(),
        ),
        out_specs=P(("groups", "ep"), None),
        check_vma=False,
    )
```

profile of v0, /device:TPU:11, one launch (start us, length us, event | category | flops | bytes accessed | tf_op | source)
XLA Modules:
  0.0 163.3 jit_solution(14443241633819949122)
XLA Ops:
  0.0 0.0 copy-start
  0.0 0.8 copy.27
  0.8 0.1 eq.55
  0.9 0.1 eq.51
  1.0 0.6 reduce-window.6
  1.6 0.2 slice_reduce_fusion
  1.9 0.1 fusion.25
  1.9 0.1 reduce_sum.52
  2.1 0.1 copy.30
  2.1 0.7 multiply_add_fusion
  2.8 0.1 fusion.19
  3.0 1.2 fusion.16
  4.1 1.7 %convolution_convert_fusion = bf16[288,2880]{1,0:T(8,128)(2,1)S(1)} fusion(pred[288,64]{0,1:T(8,128)(4,1)S(1)} %fusion.19, bf16[64,2880]{1,0:T(8,128)(2,1)} %param.8, f32[2880]{0:T(1024)} %param.11, f32[64]{0:T(128)S(1)} %add_rsqrt_fusion), kind=kOutput, calls=%fused_computation.6 | convolution fusion | flops 107735040 | bytes 2057728 | tf_op jit(solution)/shard_map/dot_general | solution.py:30
  5.8 0.0 copy-start.2
  5.8 1.7 %reshape_reshape.3 = bf16[16,18,2880]{2,1,0:T(8,128)(2,1)} reshape(bf16[288,2880]{1,0:T(8,128)(2,1)S(1)} %convolution_convert_fusion) | data formatting | bytes 3317760 | tf_op jit(solution)/shard_map/reshape;reshape | solution.py:35
  7.6 6.6 %all-to-all-start = ((bf16[16,18,2880]{2,1,0:T(8,128)(2,1)}), bf16[16,18,2880]{2,1,0:T(8,128)(2,1)S(1)}, u32[]{:S(2)}, u32[]{:S(2)}) async-start(bf16[16,18,2880]{2,1,0:T(8,128)(2,1)} %reshape_reshape.3), calls=%async_computation | async-start | bytes 4521984 | tf_op jit(solution)/shard_map/all_to_all | solution.py:36
  14.1 0.0 copy-done.2
  14.1 0.1 reduce.1
  14.2 50.9 %all-to-all-done = bf16[16,18,2880]{2,1,0:T(8,128)(2,1)S(1)} async-done(((bf16[16,18,2880]{2,1,0:T(8,128)(2,1)}), bf16[16,18,2880]{2,1,0:T(8,128)(2,1)S(1)}, u32[]{:S(2)}, u32[]{:S(2)}) %all-to-all-start) | async-done | bytes 1658912 | tf_op jit(solution)/shard_map/all_to_all | solution.py:36
  65.0 1.8 %reshape.51 = bf16[288,2880]{1,0:T(8,128)(2,1)} reshape(bf16[16,18,2880]{2,1,0:T(8,128)(2,1)S(1)} %all-to-all-done) | data formatting | bytes 3317760 | tf_op jit(solution)/shard_map/reshape | solution.py:39
  66.8 19.5 %fusion.4 = f32[288,5760]{1,0:T(8,128)} fusion(bf16[288,2880]{1,0:T(8,128)(2,1)} %reshape.51, bf16[1,2880,5760]{2,1,0:T(8,128)(2,1)} %param.12, f32[5760]{0:T(1024)S(1)} %reduce.1), kind=kOutput, calls=%fused_computation.4 | convolution fusion | flops 9556807680 | bytes 41495040 | tf_op jit(solution)/shard_map/dot_general | solution.py:41
  86.4 13.2 %fusion.7 = bf16[288,2880]{1,0:T(8,128)(2,1)S(1)} fusion(bf16[1,2880,2880]{2,1,0:T(8,128)(2,1)} %param.14, f32[288,5760]{1,0:T(8,128)} %fusion.4), kind=kOutput, calls=%fused_computation.5 | convolution fusion | flops 4785039360 | bytes 25399296 | tf_op jit(solution)/shard_map/dot_general | solution.py:49
  99.6 0.0 copy-start.4
  99.6 0.0 copy-start.3
  99.6 1.7 %reshape.52 = bf16[16,18,2880]{2,1,0:T(8,128)(2,1)} reshape(bf16[288,2880]{1,0:T(8,128)(2,1)S(1)} %fusion.7) | data formatting | bytes 3317760 | tf_op jit(solution)/shard_map/reshape | solution.py:53
  101.3 5.0 %all-to-all-start.1 = ((bf16[16,18,2880]{2,1,0:T(8,128)(2,1)}), bf16[16,18,2880]{2,1,0:T(8,128)(2,1)S(1)}, u32[]{:S(2)}, u32[]{:S(2)}) async-start(bf16[16,18,2880]{2,1,0:T(8,128)(2,1)} %reshape.52), calls=%async_computation.1 | async-start | bytes 4521984 | tf_op jit(solution)/shard_map/all_to_all | solution.py:52
  106.4 0.0 copy-done.4
  106.4 0.1 select_reduce_fusion
  106.6 50.7 %all-to-all-done.1 = bf16[16,18,2880]{2,1,0:T(8,128)(2,1)S(1)} async-done(((bf16[16,18,2880]{2,1,0:T(8,128)(2,1)}), bf16[16,18,2880]{2,1,0:T(8,128)(2,1)S(1)}, u32[]{:S(2)}, u32[]{:S(2)}) %all-to-all-start.1) | async-done | bytes 1658912 | tf_op jit(solution)/shard_map/all_to_all | solution.py:52
  157.3 1.8 %reshape.53 = bf16[288,2880]{1,0:T(8,128)(2,1)} reshape(bf16[16,18,2880]{2,1,0:T(8,128)(2,1)S(1)} %all-to-all-done.1) | data formatting | bytes 3317760 | tf_op jit(solution)/shard_map/reshape | solution.py:61
  159.1 2.6 %convolution_add_fusion.1 = f32[64,2880]{1,0:T(8,128)S(1)} fusion(f32[288,64]{0,1:T(8,128)S(1)} %select_reduce_fusion, bf16[288,2880]{1,0:T(8,128)(2,1)} %reshape.53, bf16[64,2880]{1,0:T(8,128)(2,1)S(1)} %copy-done.1), kind=kOutput, calls=%fused_computation.8 | convolution fusion | flops 637378560 | bytes 2838528 | tf_op jit(solution)/shard_map/dot_general | solution.py:62
  161.7 1.6 fusion.10
  (11 shorter events, 0.1 us)
Async XLA Ops:
  0.0 161.7 %copy-start = (f32[16,2880]{1,0:T(8,128)S(1)}, f32[16,2880]{1,0:T(8,128)}, u32[]{:S(2)}) copy-start(f32[16,2880]{1,0:T(8,128)} %param.15) | copy-start | bytes 552964
  5.8 8.3 %copy-start.2 = (f32[1,5760]{1,0:T(1,128)S(1)}, f32[1,5760]{1,0:T(1,128)}, u32[]{:S(2)}) copy-start(f32[1,5760]{1,0:T(1,128)} %param.13) | copy-start | bytes 69124
  7.6 57.5 %all-to-all-start = ((bf16[16,18,2880]{2,1,0:T(8,128)(2,1)}), bf16[16,18,2880]{2,1,0:T(8,128)(2,1)S(1)}, u32[]{:S(2)}, u32[]{:S(2)}) async-start(bf16[16,18,2880]{2,1,0:T(8,128)(2,1)} %reshape_reshape.3), calls=%async_computation | async-start | bytes 4521984 | tf_op jit(solution)/shard_map/all_to_all | solution.py:36
  99.6 6.8 %copy-start.4 = (s32[64,4]{0,1:T(4,128)S(1)}, s32[64,4]{0,1:T(4,128)}, u32[]{:S(2)}) copy-start(s32[64,4]{0,1:T(4,128)} %param.10) | copy-start | bytes 3076
  99.6 6.8 %copy-start.3 = (s32[64,4]{0,1:T(4,128)S(1)}, s32[64,4]{0,1:T(4,128)}, u32[]{:S(2)}) copy-start(s32[64,4]{0,1:T(4,128)} %param.9) | copy-start | bytes 3076
  101.3 57.8 %copy-start.1 = (bf16[64,2880]{1,0:T(8,128)(2,1)S(1)}, bf16[64,2880]{1,0:T(8,128)(2,1)}, u32[]{:S(2)}) copy-start(bf16[64,2880]{1,0:T(8,128)(2,1)} %param.8) | copy-start | bytes 1105924
  101.3 56.0 %all-to-all-start.1 = ((bf16[16,18,2880]{2,1,0:T(8,128)(2,1)}), bf16[16,18,2880]{2,1,0:T(8,128)(2,1)S(1)}, u32[]{:S(2)}, u32[]{:S(2)}) async-start(bf16[16,18,2880]{2,1,0:T(8,128)(2,1)} %reshape.52), calls=%async_computation.1 | async-start | bytes 4521984 | tf_op jit(solution)/shard_map/all_to_all | solution.py:52
where the time goes:
time: 164 us; the launch traced here: 163 us
  waiting for transfers between devices  102 us (62%)
  matrix products  38.6 us (24%)
  starting transfers between devices  11.6 us (7%)
  local copies, waits for them, and re-layouts  8.44 us (5%)
  other arithmetic  2.94 us (2%)
    all_to_all x1, waiting for transfers between devices, shards(): lax.all_to_all(outgoing, 'ep', split_axis=0, concat_axis=0, tiled=True)  50.9 us
    all_to_all x1, waiting for transfers between devices, shards(): lax.all_to_all(result.reshape(source_count, slot_count, model_width), 'ep...  50.7 us
    dot_general x1, matrix products, shards(): jnp.dot(flat_rows, weight_in[0], preferred_element_type=jnp.float32)  19.5 us
    dot_general x1, matrix products, shards(): jnp.dot(activated, weight_out[0], preferred_element_type=jnp.float32)  13.2 us
    all_to_all x1, starting transfers between devices, shards(): lax.all_to_all(outgoing, 'ep', split_axis=0, concat_axis=0, tiled=True)  6.56 us
    all_to_all x1, starting transfers between devices, shards(): lax.all_to_all(result.reshape(source_count, slot_count, model_width), 'ep...  5.05 us
  transfers between devices with their start and end apart: 2, of which 2 were waited for; matrix products, arithmetic and copies ran while one was open for 0% of the time, Pallas kernels for 0%

commit v1 on v0

v1 whole, which is shorter than its diff:
```python
import functools

import jax
import jax.numpy as jnp
from jax import lax
from jax.experimental import pallas as pl
from jax.experimental.pallas import tpu as pltpu
from jax.sharding import PartitionSpec as P

CAP = 18
LANES = 128
BLOCK = 768


def route_weights(gate_ints):
    int_gates = gate_ints.astype(jnp.float32)
    return int_gates / jnp.sum(int_gates, axis=1, keepdims=True)


def normalize(tokens, norm_gain):
    tok_float = tokens.astype(jnp.float32)
    row_scale = lax.rsqrt(jnp.mean(tok_float * tok_float, axis=1, keepdims=True) + 1e-05)
    return (tok_float * row_scale * norm_gain[None, :]).astype(jnp.bfloat16)


def exchange_shards(tokens, expert_ids, gate_ints, norm_gain, weight_in, bias_in, weight_out, bias_out):
    device_count = lax.axis_size("ep")
    expert_count = bias_out.shape[0]
    part_count = device_count // expert_count
    row_count, model_width = tokens.shape
    top_count = expert_ids.shape[1]
    capacity = CAP
    tok_float = tokens.astype(jnp.float32)
    normed = normalize(tokens, norm_gain)
    route_weight = route_weights(gate_ints)
    flat_ids = expert_ids.reshape(row_count * top_count)
    one_hot = (flat_ids[:, None] == jnp.arange(expert_count, dtype=jnp.int32)[None, :]).astype(jnp.int32)
    slot_rank = jnp.sum((jnp.cumsum(one_hot, axis=0) - one_hot) * one_hot, axis=1)
    slot_target = (flat_ids * capacity + slot_rank).reshape(row_count, top_count)
    slot_ids = jnp.arange(expert_count * capacity, dtype=jnp.int32)
    slot_match = slot_target[None, :, :] == slot_ids[:, None, None]
    picker = jnp.any(slot_match, axis=2).astype(jnp.bfloat16)
    placed = jnp.dot(picker, normed, preferred_element_type=jnp.float32).astype(jnp.bfloat16)
    combiner = jnp.transpose(jnp.sum(jnp.where(slot_match, route_weight[None, :, :], 0.0), axis=2))
    outgoing = jnp.broadcast_to(
        placed.reshape(expert_count, 1, capacity, model_width),
        (expert_count, part_count, capacity, model_width),
    ).reshape(device_count, capacity, model_width)
    arrived = lax.all_to_all(outgoing, "ep", split_axis=0, concat_axis=0, tiled=True)
    source_count, slot_count = arrived.shape[:2]
    flat_rows = arrived.reshape(source_count * slot_count, model_width)
    pre_act = jnp.dot(flat_rows, weight_in[0], preferred_element_type=jnp.float32) + bias_in[0][None, :]
    half_width = pre_act.shape[1] // 2
    gate_part = pre_act[:, :half_width]
    up_part = pre_act[:, half_width:]
    activated = (gate_part * jax.nn.sigmoid(1.702 * gate_part) * (up_part + 1.0)).astype(jnp.bfloat16)
    result = jnp.dot(activated, weight_out[0], preferred_element_type=jnp.float32).astype(jnp.bfloat16)
    returned = lax.all_to_all(
        result.reshape(source_count, slot_count, model_width), "ep", split_axis=0, concat_axis=0, tiled=True
    )
    part_sum = jnp.sum(
        returned.reshape(expert_count, part_count, capacity, model_width), axis=1, dtype=jnp.float32
    ).reshape(expert_count * capacity, model_width)
    moe_rows = jnp.dot(combiner, part_sum, precision=lax.Precision.HIGHEST)
    expert_hot = expert_ids[:, :, None] == jnp.arange(expert_count, dtype=jnp.int32)[None, None, :]
    expert_weight = jnp.sum(jnp.where(expert_hot, route_weight[:, :, None], 0.0), axis=1)
    bias_term = jnp.dot(expert_weight, bias_out, precision=lax.Precision.HIGHEST)
    return (tok_float + moe_rows + bias_term).astype(jnp.bfloat16)


def routing(tail, expert, top, slots):
    rows, width = tail.shape
    f32, bf16 = jnp.float32, jnp.bfloat16
    expert = expert.astype(f32)
    nt = (((1,), (1,)), ((), ()))
    sub = lax.broadcasted_iota(jnp.int32, (16, width), 0)
    lane = lax.broadcasted_iota(jnp.int32, (16, width), 1)
    pick_id = ((sub == lane) & (sub < top)).astype(f32).astype(bf16)
    pick_gate = ((sub + top == lane) & (sub < top)).astype(f32).astype(bf16)
    ids = lax.dot_general(pick_id, tail, nt, preferred_element_type=f32)
    gates = lax.dot_general(pick_gate, tail, nt, preferred_element_type=f32)
    entry = lax.broadcasted_iota(jnp.int32, ids.shape, 0)
    hit = jnp.where((ids == expert) & (entry < top), 1.0, 0.0)
    named = jnp.sum(hit, axis=0, keepdims=True)
    weight = jnp.sum(hit * gates, axis=0, keepdims=True) / jnp.sum(gates, axis=0, keepdims=True)
    first = lax.broadcasted_iota(jnp.int32, (rows, rows), 0)
    second = lax.broadcasted_iota(jnp.int32, (rows, rows), 1)
    upper = jnp.where(first <= second, 1.0, 0.0).astype(bf16)
    lower = jnp.where(first >= second, 1.0, 0.0).astype(bf16)
    named_wide = jnp.broadcast_to(named, (16, rows)).astype(bf16)
    count = jnp.dot(named_wide, upper, preferred_element_type=f32)[:1]
    slot = lax.broadcasted_iota(jnp.int32, (slots, rows), 0).astype(f32) + 1.0
    picker = jnp.where((count == slot) & (named > 0.5), 1.0, 0.0)
    slot_weight = jnp.sum(picker * weight, axis=1, keepdims=True)
    tail_float = tail.astype(f32)
    tail_lane = lax.broadcasted_iota(jnp.int32, tail.shape, 1)
    named_col = jnp.sum(jnp.where((tail_float == expert) & (tail_lane < top), 1.0, 0.0), axis=1, keepdims=True)
    count_col = jnp.dot(
        lower, jnp.broadcast_to(named_col, (rows, LANES)).astype(bf16), preferred_element_type=f32
    )[:, :1]
    slot_row = lax.broadcasted_iota(jnp.int32, (rows, slots), 1).astype(f32) + 1.0
    placer = jnp.where((count_col == slot_row) & (named_col > 0.5), 1.0, 0.0)
    return picker.astype(bf16), placer.astype(bf16), slot_weight


def expert_kernel(
    top, width, steps_in, expert_ref, near_ref, near_mate_ref, far_ref, far_mate_ref, win_ref, bin_ref, wout_ref,
    bout_ref, far_out, far_mate_out, near_out, near_mate_out, picked, pre, act, placers, weights,
):
    step = pl.program_id(0)
    f32, bf16 = jnp.float32, jnp.bfloat16
    half_rows = near_ref.shape[0]
    slots = picked.shape[0] // 2
    groups = ((near_ref, near_mate_ref), (far_ref, far_mate_ref))

    @pl.when(step == 0)
    def _():
        for g, (own, mate) in enumerate(groups):
            tail = jnp.concatenate([own[:, width:], mate[:, width:]], axis=0)
            picker, placer, slot_weight = routing(tail, expert_ref[0, 0], top, slots)
            placers[g] = placer
            weights[g] = slot_weight
            rows = jnp.dot(picker[:, :half_rows], own[:, :width], preferred_element_type=f32)
            rows += jnp.dot(picker[:, half_rows:], mate[:, :width], preferred_element_type=f32)
            picked[g * slots : (g + 1) * slots] = rows.astype(bf16)

    @pl.when(step < steps_in)
    def _():
        at = pl.multiple_of(step * BLOCK, BLOCK)
        pre[:, pl.ds(at, BLOCK)] = (
            jnp.dot(picked[...], win_ref[0], preferred_element_type=f32) + bin_ref[...]
        )

    @pl.when(step == steps_in)
    def _():
        for at in range(0, width, BLOCK):
            end = min(at + BLOCK, width)
            gate = pre[:, at:end]
            up = pre[:, width + at : width + end]
            act[:, at:end] = (gate * jax.nn.sigmoid(1.702 * gate) * (up + 1.0)).astype(bf16)

    @pl.when(step >= steps_in)
    def _():
        result = jnp.dot(act[...], wout_ref[0], preferred_element_type=f32) + bout_ref[...]
        for g, (own, mate) in enumerate(((near_out, near_mate_out), (far_out, far_mate_out))):
            part = (result[g * slots : (g + 1) * slots] * weights[g]).astype(bf16)
            spread = jnp.dot(placers[g], part, preferred_element_type=f32).astype(bf16)
            own[...] = spread[:half_rows]
            mate[...] = spread[half_rows:]


def run_expert(expert, blocks, top, weight_in, bias_in, weight_out, bias_row):
    half_rows, wide = blocks[0].shape
    width = weight_in.shape[1]
    hidden = weight_out.shape[1]
    slots = 2 * half_rows // 64 * CAP
    steps_in = pl.cdiv(2 * hidden, BLOCK)
    steps_out = pl.cdiv(width, BLOCK)
    whole = pl.BlockSpec((half_rows, wide), lambda j: (0, 0), pipeline_mode=pl.Buffered(1))
    first = lambda j: jnp.minimum(j, steps_in - 1)
    second = lambda j: jnp.maximum(j - steps_in, 0)
    out = pl.BlockSpec((half_rows, BLOCK), lambda j: (0, second(j)))
    return pl.pallas_call(
        functools.partial(expert_kernel, top, width, steps_in),
        grid=(steps_in + steps_out,),
        in_specs=[
            pl.BlockSpec(memory_space=pltpu.SMEM),
            whole, whole, whole, whole,
            pl.BlockSpec((1, width, BLOCK), lambda j: (0, 0, first(j))),
            pl.BlockSpec((1, BLOCK), lambda j: (0, first(j))),
            pl.BlockSpec((1, hidden, BLOCK), lambda j: (0, 0, second(j))),
            pl.BlockSpec((1, BLOCK), lambda j: (0, second(j))),
        ],
        out_specs=[out] * 4,
        out_shape=[jax.ShapeDtypeStruct((half_rows, width), jnp.bfloat16)] * 4,
        scratch_shapes=[
            pltpu.VMEM((2 * slots, width), jnp.bfloat16),
            pltpu.VMEM((2 * slots, steps_in * BLOCK), jnp.float32),
            pltpu.VMEM((2 * slots, hidden), jnp.bfloat16),
            pltpu.VMEM((2, 2 * half_rows, slots), jnp.bfloat16),
            pltpu.VMEM((2, slots, 1), jnp.float32),
        ],
        compiler_params=pltpu.CompilerParams(vmem_limit_bytes=48 * 2**20),
    )(expert, *blocks, weight_in, bias_in, weight_out, bias_row)


def ring_shards(tokens, expert_ids, gate_ints, norm_gain, weight_in, bias_in, weight_out, bias_out):
    device_count = lax.axis_size("ep")
    chips = device_count // 2
    reach = chips // 2
    ring = list(range(0, chips, 2)) + list(range(chips - 1, 0, -2))
    right = [(ring[i] * 2 + k, ring[(i + 1) % chips] * 2 + k) for i in range(chips) for k in range(2)]
    left = [(b, a) for a, b in right]
    mate = [(i, i ^ 1) for i in range(device_count)]
    send = lambda value, pairs: lax.ppermute(value, "ep", pairs)
    bf16, f32 = jnp.bfloat16, jnp.float32
    row_count, width = tokens.shape
    top = expert_ids.shape[1]
    half = row_count // 2
    spare = -width % LANES
    normed = normalize(tokens, norm_gain)
    block = jnp.concatenate(
        [normed, expert_ids.astype(bf16), gate_ints.astype(bf16), jnp.zeros((row_count, spare - 2 * top), bf16)],
        axis=1,
    )
    seen = {0: block}
    from_left = from_right = block
    for hop in range(1, reach):
        from_left, from_right = send(from_left, right), send(from_right, left)
        seen[-hop], seen[hop] = from_left, from_right
    low, high = send(from_left[:half], right), send(from_right[half:], left)
    near = jnp.concatenate([seen[0], seen[-1], seen[1], seen[-2]], axis=0)
    far = jnp.concatenate([seen[2], seen[-3], seen[3], low, high], axis=0)
    near_mate, far_mate = send(near, mate), send(far, mate)
    me = lax.axis_index("ep")
    bias_row = lax.dynamic_slice_in_dim(bias_out, me, 1, axis=0)
    far_sum, far_sum_mate, near_sum, near_sum_mate = run_expert(
        me.astype(jnp.int32).reshape(1, 1), (near, near_mate, far, far_mate), top, weight_in, bias_in, weight_out, bias_row
    )
    add = lambda a, b: (a.astype(f32) + b.astype(f32)).astype(bf16)
    far_sum = add(far_sum, send(far_sum_mate, mate))
    near_sum = add(near_sum, send(near_sum_mate, mate))
    cut = lambda value, i: value[i * row_count : (i + 1) * row_count]
    owed = {2: cut(far_sum, 0), -3: cut(far_sum, 1), 3: cut(far_sum, 2), 4: cut(far_sum, 3)}
    owed |= {0: cut(near_sum, 0), -1: cut(near_sum, 1), 1: cut(near_sum, 2), -2: cut(near_sum, 3)}
    up, down = send(owed[4][:half], right), send(owed[4][half:], left)
    up = jnp.concatenate([add(owed[3][:half], up), owed[3][half:]], axis=0)
    down = jnp.concatenate([owed[-3][:half], add(owed[-3][half:], down)], axis=0)
    for hop in range(reach - 2, 0, -1):
        up, down = add(owed[hop], send(up, right)), add(owed[-hop], send(down, left))
    up, down = send(up, right), send(down, left)
    moe = owed[0].astype(f32) + up.astype(f32) + down.astype(f32)
    return (tokens.astype(f32) + moe).astype(bf16)


def solution(mesh):
    ep = mesh.shape["ep"]

    def shards(*arrays):
        whole_experts = arrays[-1].shape[0] == ep and ep == 16
        return (ring_shards if whole_experts else exchange_shards)(*arrays)

    return jax.shard_map(
        shards,
        mesh=mesh,
        in_specs=(
            P(("groups", "ep"), None),
            P(("groups", "ep"), None),
            P(("groups", "ep"), None),
            P(),
            P("ep", None, None),
            P("ep", None),
            P("ep", None, None),
            P(),
        ),
        out_specs=P(("groups", "ep"), None),
        check_vma=False,
    )
```

time: 164 us -> 140 us (0.85)
  the two profiles are of different devices: /device:TPU:11 before, /device:TPU:0 now
where the time goes in v1:
time: 140 us; the launch traced here: 139 us
  waiting for transfers between devices  63.2 us (45%)
  Pallas kernels  34.8 us (25%)
  starting transfers between devices  19 us (14%)
  local copies, waits for them, and re-layouts  12.5 us (9%)
  other arithmetic  9.31 us (7%)
    ppermute x20, waiting for transfers between devices, ring_shards(): send = lambda value, pairs: lax.ppermute(value, 'ep', pairs)  63.2 us
    pallas_call x1, Pallas kernels, run_expert(): pl.pallas_call(functools.partial(expert_kernel, top, width, steps_in), gr...  34.8 us
    ppermute x20, starting transfers between devices, ring_shards(): send = lambda value, pairs: lax.ppermute(value, 'ep', pairs)  19 us
    pallas_call x2, local copies, waits for them, and re-layouts, run_expert(): pl.pallas_call(functools.partial(expert_kernel, top, width, steps_in), gr...  5.23 us
    ppermute x2, local copies, waits for them, and re-layouts, ring_shards(): send = lambda value, pairs: lax.ppermute(value, 'ep', pairs)  4.37 us
    convert_element_type x6, other arithmetic, ring_shards(): add = lambda a, b: (a.astype(f32) + b.astype(f32)).astype(bf16)  3.73 us
  transfers between devices with their start and end apart: 20, of which 12 were waited for; matrix products, arithmetic and copies ran while one was open for 8% of the time, Pallas kernels for 0%

profile of v1, /device:TPU:0, one launch (start us, length us, event | category | flops | bytes accessed | tf_op | source)
XLA Modules:
  0.0 139.1 jit_solution(8063119890003622352)
XLA Ops:
  0.0 1.2 fusion
  2.8 1.2 fusion.2
  4.1 3.0 %collective-permute-start.1 = (bf16[64,2944]{1,0:T(8,128)(2,1)S(1)}, bf16[64,2944]{1,0:T(8,128)(2,1)S(1)}, u32[]{:S(2)}, u32[]{:S(2)}) collective-permute-start(bf16[64,2944]{1,0:T(8,128)(2,1)S(1)} %concatenate.15), channel_id=1, source_target_pairs={{4,0},{5,1},{8,4},{9,5},{12,8},{13,9},{14,12},{15,13},{10,14},{11,... | collective-permute-start | bytes 1130504 | tf_op jit(solution)/shard_map/ppermute | solution.py:195
  7.3 8.7 %collective-permute-done.1 = bf16[64,2944]{1,0:T(8,128)(2,1)S(1)} collective-permute-done((bf16[64,2944]{1,0:T(8,128)(2,1)S(1)}, bf16[64,2944]{1,0:T(8,128)(2,1)S(1)}, u32[]{:S(2)}, u32[]{:S(2)}) %collective-permute-start.1) | collective-permute-done | bytes 376864 | tf_op jit(solution)/shard_map/ppermute | solution.py:195
  16.0 1.7 %collective-permute-start.4 = (bf16[64,2944]{1,0:T(8,128)(2,1)S(1)}, bf16[64,2944]{1,0:T(8,128)(2,1)S(1)}, u32[]{:S(2)}, u32[]{:S(2)}) collective-permute-start(bf16[64,2944]{1,0:T(8,128)(2,1)S(1)} %collective-permute-done.1), channel_id=1, source_target_pairs={{4,0},{5,1},{8,4},{9,5},{12,8},{13,9},{14,12},{15,13},{10,14},{11,... | collective-permute-start | bytes 1130504 | tf_op jit(solution)/shard_map/ppermute | solution.py:195
  18.0 7.9 %collective-permute-done.4 = bf16[64,2944]{1,0:T(8,128)(2,1)S(1)} collective-permute-done((bf16[64,2944]{1,0:T(8,128)(2,1)S(1)}, bf16[64,2944]{1,0:T(8,128)(2,1)S(1)}, u32[]{:S(2)}, u32[]{:S(2)}) %collective-permute-start.4) | collective-permute-done | bytes 376864 | tf_op jit(solution)/shard_map/ppermute | solution.py:195
  25.9 1.3 collective-permute-start.6
  28.2 6.7 %collective-permute-done.6 = bf16[64,2944]{1,0:T(8,128)(2,1)S(1)} collective-permute-done((bf16[64,2944]{1,0:T(8,128)(2,1)S(1)}, bf16[64,2944]{1,0:T(8,128)(2,1)S(1)}, u32[]{:S(2)}, u32[]{:S(2)}) %collective-permute-start.6) | collective-permute-done | bytes 376864 | tf_op jit(solution)/shard_map/ppermute | solution.py:195
  35.0 1.2 collective-permute-start.8
  37.2 4.6 %collective-permute-done.7 = bf16[32,2944]{1,0:T(8,128)(2,1)S(1)} collective-permute-done((bf16[32,2944]{1,0:T(8,128)(2,1)S(1)}, bf16[32,2944]{1,0:T(8,128)(2,1)S(1)}, u32[]{:S(2)}, u32[]{:S(2)}) %collective-permute-start.7) | collective-permute-done | bytes 188448 | tf_op jit(solution)/shard_map/ppermute | solution.py:195
  42.0 3.4 %collective-permute-done.9.far_mate_ref = bf16[256,2944]{1,0:T(8,128)(2,1)} collective-permute-done((bf16[256,2944]{1,0:T(8,128)(2,1)S(1)}, bf16[256,2944]{1,0:T(8,128)(2,1)}, u32[]{:S(2)}, u32[]{:S(2)}) %collective-permute-start.9) | collective-permute-done | bytes 1507360 | tf_op jit(solution)/shard_map/ppermute | solution.py:195
  45.4 34.8 %shard_map.82 = (bf16[256,2880]{1,0:T(8,128)(2,1)S(1)}, bf16[256,2880]{1,0:T(8,128)(2,1)S(1)}, bf16[256,2880]{1,0:T(8,128)(2,1)S(1)}, bf16[256,2880]{1,0:T(8,128)(2,1)S(1)}) custom-call(s32[1,1]{1,0:T(1,128)} %bitcast.expert_ref, bf16[256,2944]{1,0:T(8,128)(2,1)} %copy-done.6, bf16[256,2944]{1,0:T(8,128)(2,1)} %collective-permute-done.3.near_mate_ref, ...), custom_call_target="tpu_custom_call" | custom-call | tf_op jit(solution)/shard_map/pallas_call | solution.py:163
  80.3 1.1 copy-done.2
  81.4 1.2 copy-done.3
  82.5 2.6 %copy.15 = bf16[256,2880]{0,1:T(8,128)(2,1)} copy(bf16[256,2880]{1,0:T(8,128)(2,1)} %copy-done.3) | data formatting | bytes 2949120 | tf_op jit(solution)/shard_map/pallas_call | solution.py:163
  85.3 2.6 %copy.13 = bf16[256,2880]{0,1:T(8,128)(2,1)} copy(bf16[256,2880]{1,0:T(8,128)(2,1)} %copy-done.2) | data formatting | bytes 2949120 | tf_op jit(solution)/shard_map/pallas_call | solution.py:163
  88.7 2.6 %copy.16 = bf16[256,2880]{1,0:T(8,128)(2,1)} copy(bf16[256,2880]{0,1:T(8,128)(2,1)} %collective-permute-done.11) | data formatting | bytes 2949120 | tf_op jit(solution)/shard_map/ppermute | solution.py:195
  91.3 1.8 %add_convert_fusion = bf16[256,2880]{1,0:T(8,128)(2,1)S(1)} fusion(bf16[256,2880]{1,0:T(8,128)(2,1)} %copy.16, bf16[256,2880]{1,0:T(8,128)(2,1)S(1)} %get-tuple-element.11), kind=kLoop, calls=%fused_computation | loop fusion | flops 2949120 | bytes 4423680 | tf_op jit(solution)/shard_map/convert_element_type | solution.py:220
  93.2 0.9 collective-permute-start.12
  94.1 1.1 collective-permute-start.16
  95.3 4.8 %collective-permute-done.12 = bf16[32,2880]{1,0:T(8,128)(2,1)S(1)} collective-permute-done((bf16[32,2880]{1,0:T(8,128)(2,1)S(1)}, bf16[32,2880]{1,0:T(8,128)(2,1)S(1)}, u32[]{:S(2)}, u32[]{:S(2)}) %collective-permute-start.12) | collective-permute-done | bytes 184352 | tf_op jit(solution)/shard_map/ppermute | solution.py:195
  101.5 1.2 collective-permute-start.13
  102.7 1.8 %copy.14 = bf16[256,2880]{1,0:T(8,128)(2,1)S(1)} copy(bf16[256,2880]{0,1:T(8,128)(2,1)} %collective-permute-done.10) | data formatting | bytes 2949120 | tf_op jit(solution)/shard_map/ppermute | solution.py:195
  105.4 6.0 %collective-permute-done.13 = bf16[64,2880]{1,0:T(8,128)(2,1)} collective-permute-done((bf16[64,2880]{1,0:T(8,128)(2,1)}, bf16[64,2880]{1,0:T(8,128)(2,1)}, u32[]{:S(2)}, u32[]{:S(2)}) %collective-permute-start.13) | collective-permute-done | bytes 368672 | tf_op jit(solution)/shard_map/ppermute | solution.py:195
  111.4 1.2 add_convert_fusion.5
  112.6 1.3 collective-permute-start.14
  114.3 7.1 %collective-permute-done.14 = bf16[64,2880]{1,0:T(8,128)(2,1)S(1)} collective-permute-done((bf16[64,2880]{1,0:T(8,128)(2,1)S(1)}, bf16[64,2880]{1,0:T(8,128)(2,1)S(1)}, u32[]{:S(2)}, u32[]{:S(2)}) %collective-permute-start.14) | collective-permute-done | bytes 368672 | tf_op jit(solution)/shard_map/ppermute | solution.py:195
  121.6 1.5 %collective-permute-start.18 = (bf16[64,2880]{1,0:T(8,128)(2,1)S(1)}, bf16[64,2880]{1,0:T(8,128)(2,1)S(1)}, u32[]{:S(2)}, u32[]{:S(2)}) collective-permute-start(bf16[64,2880]{1,0:T(8,128)(2,1)S(1)} %get-tuple-element.14), channel_id=1, source_target_pairs={{4,0},{5,1},{8,4},{9,5},{12,8},{13,9},{14,12},{15,13},{10,14},{11,... | collective-permute-start | bytes 1105928 | tf_op jit(solution)/shard_map/ppermute | solution.py:195
  123.7 6.7 %collective-permute-done.18 = bf16[64,2880]{1,0:T(8,128)(2,1)S(1)} collective-permute-done((bf16[64,2880]{1,0:T(8,128)(2,1)S(1)}, bf16[64,2880]{1,0:T(8,128)(2,1)S(1)}, u32[]{:S(2)}, u32[]{:S(2)}) %collective-permute-start.18) | collective-permute-done | bytes 368672 | tf_op jit(solution)/shard_map/ppermute | solution.py:195
  130.5 1.5 %collective-permute-start.19 = (bf16[64,2880]{1,0:T(8,128)(2,1)S(1)}, bf16[64,2880]{1,0:T(8,128)(2,1)S(1)}, u32[]{:S(2)}, u32[]{:S(2)}) collective-permute-start(bf16[64,2880]{1,0:T(8,128)(2,1)S(1)} %add_convert_fusion.2), channel_id=1, source_target_pairs={{4,0},{5,1},{8,4},{9,5},{12,8},{13,9},{14,12},{15,13},{10,14},{11,... | collective-permute-start | bytes 1105928 | tf_op jit(solution)/shard_map/ppermute | solution.py:195
  132.1 6.1 %collective-permute-done.19 = bf16[64,2880]{1,0:T(8,128)(2,1)S(1)} collective-permute-done((bf16[64,2880]{1,0:T(8,128)(2,1)S(1)}, bf16[64,2880]{1,0:T(8,128)(2,1)S(1)}, u32[]{:S(2)}, u32[]{:S(2)}) %collective-permute-start.19) | collective-permute-done | bytes 368672 | tf_op jit(solution)/shard_map/ppermute | solution.py:195
  138.2 0.9 fusion.3
  (59 shorter events, 8.9 us)
Async XLA Ops:
  0.0 42.0 %copy-start = (f32[16,2880]{1,0:T(8,128)S(1)}, f32[16,2880]{1,0:T(8,128)}, u32[]{:S(2)}) copy-start(f32[16,2880]{1,0:T(8,128)} %param.15) | copy-start | bytes 552964
  4.1 11.8 %collective-permute-start.1 = (bf16[64,2944]{1,0:T(8,128)(2,1)S(1)}, bf16[64,2944]{1,0:T(8,128)(2,1)S(1)}, u32[]{:S(2)}, u32[]{:S(2)}) collective-permute-start(bf16[64,2944]{1,0:T(8,128)(2,1)S(1)} %concatenate.15), channel_id=1, source_target_pairs={{4,0},{5,1},{8,4},{9,5},{12,8},{13,9},{14,12},{15,13},{10,14},{11,... | collective-permute-start | bytes 1130504 | tf_op jit(solution)/shard_map/ppermute | solution.py:195
  7.1 10.5 %collective-permute-start = (bf16[64,2944]{1,0:T(8,128)(2,1)S(1)}, bf16[64,2944]{1,0:T(8,128)(2,1)S(1)}, u32[]{:S(2)}, u32[]{:S(2)}) collective-permute-start(bf16[64,2944]{1,0:T(8,128)(2,1)S(1)} %concatenate.15), channel_id=1, source_target_pairs={{0,4},{1,5},{4,8},{5,9},{8,12},{9,13},{12,14},{13,15},{14,10},{15,... | collective-permute-start | bytes 1130504 | tf_op jit(solution)/shard_map/ppermute | solution.py:195
  16.0 9.9 %collective-permute-start.4 = (bf16[64,2944]{1,0:T(8,128)(2,1)S(1)}, bf16[64,2944]{1,0:T(8,128)(2,1)S(1)}, u32[]{:S(2)}, u32[]{:S(2)}) collective-permute-start(bf16[64,2944]{1,0:T(8,128)(2,1)S(1)} %collective-permute-done.1), channel_id=1, source_target_pairs={{4,0},{5,1},{8,4},{9,5},{12,8},{13,9},{14,12},{15,13},{10,14},{11,... | collective-permute-start | bytes 1130504 | tf_op jit(solution)/shard_map/ppermute | solution.py:195
  17.6 9.6 %collective-permute-start.2 = (bf16[64,2944]{1,0:T(8,128)(2,1)S(1)}, bf16[64,2944]{1,0:T(8,128)(2,1)S(1)}, u32[]{:S(2)}, u32[]{:S(2)}) collective-permute-start(bf16[64,2944]{1,0:T(8,128)(2,1)S(1)} %collective-permute-done), channel_id=1, source_target_pairs={{0,4},{1,5},{4,8},{5,9},{8,12},{9,13},{12,14},{13,15},{14,10},{15,... | collective-permute-start | bytes 1130504 | tf_op jit(solution)/shard_map/ppermute | solution.py:195
  25.9 9.0 %collective-permute-start.6 = (bf16[64,2944]{1,0:T(8,128)(2,1)S(1)}, bf16[64,2944]{1,0:T(8,128)(2,1)S(1)}, u32[]{:S(2)}, u32[]{:S(2)}) collective-permute-start(bf16[64,2944]{1,0:T(8,128)(2,1)S(1)} %collective-permute-done.4), channel_id=1, source_target_pairs={{4,0},{5,1},{8,4},{9,5},{12,8},{13,9},{14,12},{15,13},{10,14},{11,... | collective-permute-start | bytes 1130504 | tf_op jit(solution)/shard_map/ppermute | solution.py:195
  27.2 8.9 %collective-permute-start.5 = (bf16[64,2944]{1,0:T(8,128)(2,1)S(1)}, bf16[64,2944]{1,0:T(8,128)(2,1)S(1)}, u32[]{:S(2)}, u32[]{:S(2)}) collective-permute-start(bf16[64,2944]{1,0:T(8,128)(2,1)S(1)} %collective-permute-done.2), channel_id=1, source_target_pairs={{0,4},{1,5},{4,8},{5,9},{8,12},{9,13},{12,14},{13,15},{14,10},{15,... | collective-permute-start | bytes 1130504 | tf_op jit(solution)/shard_map/ppermute | solution.py:195
  28.0 9.1 %copy-start.6 = (bf16[256,2944]{1,0:T(8,128)(2,1)}, bf16[256,2944]{1,0:T(8,128)(2,1)S(1)}, u32[]{:S(2)}) copy-start(bf16[256,2944]{1,0:T(8,128)(2,1)S(1)} %pad_maximum_fusion.near_ref) | copy-start | bytes 4521988
  28.1 14.0 %collective-permute-start.3 = (bf16[256,2944]{1,0:T(8,128)(2,1)S(1)}, bf16[256,2944]{1,0:T(8,128)(2,1)}, u32[]{:S(2)}, u32[]{:S(2)}) collective-permute-start(bf16[256,2944]{1,0:T(8,128)(2,1)S(1)} %pad_maximum_fusion.near_ref), channel_id=1, source_target_pairs={{0,1},{1,0},{2,3},{3,2},{4,5},{5,4},{6,7},{7,6},{8,9},{9,8},{10,11... | collective-permute-start | bytes 4521992 | tf_op jit(solution)/shard_map/ppermute | solution.py:195
  28.2 17.2 %copy-start.4 = (f32[1,5760]{1,0:T(1,128)S(1)}, f32[1,5760]{1,0:T(1,128)}, u32[]{:S(2)}) copy-start(f32[1,5760]{1,0:T(1,128)} %bin_ref.1) | copy-start | bytes 69124
  35.0 6.9 %collective-permute-start.8 = (bf16[32,2944]{1,0:T(8,128)(2,1)S(1)}, bf16[32,2944]{1,0:T(8,128)(2,1)S(1)}, u32[]{:S(2)}, u32[]{:S(2)}) collective-permute-start(bf16[32,2944]{1,0:T(8,128)(2,1)S(1)} %slice.62), channel_id=1, source_target_pairs={{4,0},{5,1},{8,4},{9,5},{12,8},{13,9},{14,12},{15,13},{10,14},{11,... | collective-permute-start | bytes 565256 | tf_op jit(solution)/shard_map/ppermute | solution.py:195
  36.2 5.6 %collective-permute-start.7 = (bf16[32,2944]{1,0:T(8,128)(2,1)S(1)}, bf16[32,2944]{1,0:T(8,128)(2,1)S(1)}, u32[]{:S(2)}, u32[]{:S(2)}) collective-permute-start(bf16[32,2944]{1,0:T(8,128)(2,1)S(1)} %slice.61), channel_id=1, source_target_pairs={{0,4},{1,5},{4,8},{5,9},{8,12},{9,13},{12,14},{13,15},{14,10},{15,... | collective-permute-start | bytes 565256 | tf_op jit(solution)/shard_map/ppermute | solution.py:195
  41.9 3.5 %copy-start.8 = (bf16[256,2944]{1,0:T(8,128)(2,1)}, bf16[256,2944]{1,0:T(8,128)(2,1)S(1)}, u32[]{:S(2)}) copy-start(bf16[256,2944]{1,0:T(8,128)(2,1)S(1)} %constant_dynamic-update-slice_fusion.far_ref) | copy-start | bytes 4521988
  41.9 3.5 %collective-permute-start.9 = (bf16[256,2944]{1,0:T(8,128)(2,1)S(1)}, bf16[256,2944]{1,0:T(8,128)(2,1)}, u32[]{:S(2)}, u32[]{:S(2)}) collective-permute-start(bf16[256,2944]{1,0:T(8,128)(2,1)S(1)} %constant_dynamic-update-slice_fusion.far_ref), channel_id=1, source_target_pairs={{0,1},{1,0},{2,3},{3,2},{4,5},{5,4},{6,7},{7,6},{8,9},{9,8},{10,11... | collective-permute-start | bytes 4521992 | tf_op jit(solution)/shard_map/ppermute | solution.py:195
  80.2 1.1 copy-start.2
  81.4 1.2 copy-start.3
  85.1 3.6 %collective-permute-start.11 = (bf16[256,2880]{0,1:T(8,128)(2,1)}, bf16[256,2880]{0,1:T(8,128)(2,1)}, u32[]{:S(2)}, u32[]{:S(2)}) collective-permute-start(bf16[256,2880]{0,1:T(8,128)(2,1)} %copy.15), channel_id=1, source_target_pairs={{0,1},{1,0},{2,3},{3,2},{4,5},{5,4},{6,7},{7,6},{8,9},{9,8},{10,11... | collective-permute-start | bytes 4423688 | tf_op jit(solution)/shard_map/ppermute | solution.py:195
  87.9 14.8 %collective-permute-start.10 = (bf16[256,2880]{0,1:T(8,128)(2,1)}, bf16[256,2880]{0,1:T(8,128)(2,1)}, u32[]{:S(2)}, u32[]{:S(2)}) collective-permute-start(bf16[256,2880]{0,1:T(8,128)(2,1)} %copy.13), channel_id=1, source_target_pairs={{0,1},{1,0},{2,3},{3,2},{4,5},{5,4},{6,7},{7,6},{8,9},{9,8},{10,11... | collective-permute-start | bytes 4423688 | tf_op jit(solution)/shard_map/ppermute | solution.py:195
  93.1 8.4 %copy-start.5 = (bf16[256,2880]{1,0:T(8,128)(2,1)}, bf16[256,2880]{1,0:T(8,128)(2,1)S(1)}, u32[]{:S(2)}) copy-start(bf16[256,2880]{1,0:T(8,128)(2,1)S(1)} %add_convert_fusion) | copy-start | bytes 4423684
  93.2 6.8 %collective-permute-start.12 = (bf16[32,2880]{1,0:T(8,128)(2,1)S(1)}, bf16[32,2880]{1,0:T(8,128)(2,1)S(1)}, u32[]{:S(2)}, u32[]{:S(2)}) collective-permute-start(bf16[32,2880]{1,0:T(8,128)(2,1)S(1)} %get-tuple-element.17), channel_id=1, source_target_pairs={{0,4},{1,5},{4,8},{5,9},{8,12},{9,13},{12,14},{13,15},{14,10},{15,... | collective-permute-start | bytes 552968 | tf_op jit(solution)/shard_map/ppermute | solution.py:195
  94.1 6.5 %collective-permute-start.16 = (bf16[32,2880]{1,0:T(8,128)(2,1)S(1)}, bf16[32,2880]{1,0:T(8,128)(2,1)S(1)}, u32[]{:S(2)}, u32[]{:S(2)}) collective-permute-start(bf16[32,2880]{1,0:T(8,128)(2,1)S(1)} %get-tuple-element.18), channel_id=1, source_target_pairs={{4,0},{5,1},{8,4},{9,5},{12,8},{13,9},{14,12},{15,13},{10,14},{11,... | collective-permute-start | bytes 552968 | tf_op jit(solution)/shard_map/ppermute | solution.py:195
  101.5 10.0 %collective-permute-start.13 = (bf16[64,2880]{1,0:T(8,128)(2,1)}, bf16[64,2880]{1,0:T(8,128)(2,1)}, u32[]{:S(2)}, u32[]{:S(2)}) collective-permute-start(bf16[64,2880]{1,0:T(8,128)(2,1)} %pad_maximum_fusion.1), channel_id=1, source_target_pairs={{0,4},{1,5},{4,8},{5,9},{8,12},{9,13},{12,14},{13,15},{14,10},{15,... | collective-permute-start | bytes 1105928 | tf_op jit(solution)/shard_map/ppermute | solution.py:195
  104.6 9.7 %collective-permute-start.17 = (bf16[64,2880]{1,0:T(8,128)(2,1)S(1)}, bf16[64,2880]{1,0:T(8,128)(2,1)S(1)}, u32[]{:S(2)}, u32[]{:S(2)}) collective-permute-start(bf16[64,2880]{1,0:T(8,128)(2,1)S(1)} %pad_maximum_fusion.2), channel_id=1, source_target_pairs={{4,0},{5,1},{8,4},{9,5},{12,8},{13,9},{14,12},{15,13},{10,14},{11,... | collective-permute-start | bytes 1105928 | tf_op jit(solution)/shard_map/ppermute | solution.py:195
  112.6 8.8 %collective-permute-start.14 = (bf16[64,2880]{1,0:T(8,128)(2,1)S(1)}, bf16[64,2880]{1,0:T(8,128)(2,1)S(1)}, u32[]{:S(2)}, u32[]{:S(2)}) collective-permute-start(bf16[64,2880]{1,0:T(8,128)(2,1)S(1)} %add_convert_fusion.5), channel_id=1, source_target_pairs={{0,4},{1,5},{4,8},{5,9},{8,12},{9,13},{12,14},{13,15},{14,10},{15,... | collective-permute-start | bytes 1105928 | tf_op jit(solution)/shard_map/ppermute | solution.py:195
  114.3 23.9 %copy-start.7 = (bf16[64,2880]{1,0:T(8,128)(2,1)S(1)}, bf16[64,2880]{1,0:T(8,128)(2,1)}, u32[]{:S(2)}) copy-start(bf16[64,2880]{1,0:T(8,128)(2,1)} %param.8) | copy-start | bytes 1105924
  121.6 8.8 %collective-permute-start.18 = (bf16[64,2880]{1,0:T(8,128)(2,1)S(1)}, bf16[64,2880]{1,0:T(8,128)(2,1)S(1)}, u32[]{:S(2)}, u32[]{:S(2)}) collective-permute-start(bf16[64,2880]{1,0:T(8,128)(2,1)S(1)} %get-tuple-element.14), channel_id=1, source_target_pairs={{4,0},{5,1},{8,4},{9,5},{12,8},{13,9},{14,12},{15,13},{10,14},{11,... | collective-permute-start | bytes 1105928 | tf_op jit(solution)/shard_map/ppermute | solution.py:195
  123.1 16.0 %copy-start.1 = (f32[16,2880]{1,0:T(8,128)S(1)}, f32[16,2880]{1,0:T(8,128)}, u32[]{:S(2)}) copy-start(f32[16,2880]{1,0:T(8,128)} %param.15) | copy-start | bytes 552964
  123.1 8.9 %collective-permute-start.15 = (bf16[64,2880]{1,0:T(8,128)(2,1)S(1)}, bf16[64,2880]{1,0:T(8,128)(2,1)S(1)}, u32[]{:S(2)}, u32[]{:S(2)}) collective-permute-start(bf16[64,2880]{1,0:T(8,128)(2,1)S(1)} %get-tuple-element.13), channel_id=1, source_target_pairs={{0,4},{1,5},{4,8},{5,9},{8,12},{9,13},{12,14},{13,15},{14,10},{15,... | collective-permute-start | bytes 1105928 | tf_op jit(solution)/shard_map/ppermute | solution.py:195
  130.5 7.7 %collective-permute-start.19 = (bf16[64,2880]{1,0:T(8,128)(2,1)S(1)}, bf16[64,2880]{1,0:T(8,128)(2,1)S(1)}, u32[]{:S(2)}, u32[]{:S(2)}) collective-permute-start(bf16[64,2880]{1,0:T(8,128)(2,1)S(1)} %add_convert_fusion.2), channel_id=1, source_target_pairs={{4,0},{5,1},{8,4},{9,5},{12,8},{13,9},{14,12},{15,13},{10,14},{11,... | collective-permute-start | bytes 1105928 | tf_op jit(solution)/shard_map/ppermute | solution.py:195

commit v2 on v0

v2 whole, which is shorter than its diff:
```python
import functools

import jax
import jax.numpy as jnp
from jax import lax
from jax.experimental import pallas as pl
from jax.experimental.pallas import tpu as pltpu
from jax.sharding import PartitionSpec as P

CAP = 18
LANES = 128
BLOCK = 768


def route_weights(gate_ints):
    int_gates = gate_ints.astype(jnp.float32)
    return int_gates / jnp.sum(int_gates, axis=1, keepdims=True)


def normalize(tokens, norm_gain):
    tok_float = tokens.astype(jnp.float32)
    row_scale = lax.rsqrt(jnp.mean(tok_float * tok_float, axis=1, keepdims=True) + 1e-05)
    return (tok_float * row_scale * norm_gain[None, :]).astype(jnp.bfloat16)


def exchange_shards(tokens, expert_ids, gate_ints, norm_gain, weight_in, bias_in, weight_out, bias_out):
    device_count = lax.axis_size("ep")
    expert_count = bias_out.shape[0]
    part_count = device_count // expert_count
    row_count, model_width = tokens.shape
    top_count = expert_ids.shape[1]
    capacity = CAP
    tok_float = tokens.astype(jnp.float32)
    normed = normalize(tokens, norm_gain)
    route_weight = route_weights(gate_ints)
    flat_ids = expert_ids.reshape(row_count * top_count)
    one_hot = (flat_ids[:, None] == jnp.arange(expert_count, dtype=jnp.int32)[None, :]).astype(jnp.int32)
    slot_rank = jnp.sum((jnp.cumsum(one_hot, axis=0) - one_hot) * one_hot, axis=1)
    slot_target = (flat_ids * capacity + slot_rank).reshape(row_count, top_count)
    slot_ids = jnp.arange(expert_count * capacity, dtype=jnp.int32)
    slot_match = slot_target[None, :, :] == slot_ids[:, None, None]
    picker = jnp.any(slot_match, axis=2).astype(jnp.bfloat16)
    placed = jnp.dot(picker, normed, preferred_element_type=jnp.float32).astype(jnp.bfloat16)
    combiner = jnp.transpose(jnp.sum(jnp.where(slot_match, route_weight[None, :, :], 0.0), axis=2))
    outgoing = jnp.broadcast_to(
        placed.reshape(expert_count, 1, capacity, model_width),
        (expert_count, part_count, capacity, model_width),
    ).reshape(device_count, capacity, model_width)
    arrived = lax.all_to_all(outgoing, "ep", split_axis=0, concat_axis=0, tiled=True)
    source_count, slot_count = arrived.shape[:2]
    flat_rows = arrived.reshape(source_count * slot_count, model_width)
    pre_act = jnp.dot(flat_rows, weight_in[0], preferred_element_type=jnp.float32) + bias_in[0][None, :]
    half_width = pre_act.shape[1] // 2
    gate_part = pre_act[:, :half_width]
    up_part = pre_act[:, half_width:]
    activated = (gate_part * jax.nn.sigmoid(1.702 * gate_part) * (up_part + 1.0)).astype(jnp.bfloat16)
    result = jnp.dot(activated, weight_out[0], preferred_element_type=jnp.float32).astype(jnp.bfloat16)
    returned = lax.all_to_all(
        result.reshape(source_count, slot_count, model_width), "ep", split_axis=0, concat_axis=0, tiled=True
    )
    part_sum = jnp.sum(
        returned.reshape(expert_count, part_count, capacity, model_width), axis=1, dtype=jnp.float32
    ).reshape(expert_count * capacity, model_width)
    moe_rows = jnp.dot(combiner, part_sum, precision=lax.Precision.HIGHEST)
    expert_hot = expert_ids[:, :, None] == jnp.arange(expert_count, dtype=jnp.int32)[None, None, :]
    expert_weight = jnp.sum(jnp.where(expert_hot, route_weight[:, :, None], 0.0), axis=1)
    bias_term = jnp.dot(expert_weight, bias_out, precision=lax.Precision.HIGHEST)
    return (tok_float + moe_rows + bias_term).astype(jnp.bfloat16)


def norm_kernel(top, tokens_ref, ids_ref, gates_ref, gain_ref, *out_refs):
    f32, bf16 = jnp.float32, jnp.bfloat16
    rows, width = tokens_ref.shape
    tok = tokens_ref[...].astype(f32)
    scale = lax.rsqrt(jnp.mean(tok * tok, axis=1, keepdims=True) + 1e-05)
    normed = (tok * scale * gain_ref[...]).astype(bf16)
    spare = sum(ref.shape[1] for ref in out_refs) - width
    sub = lax.broadcasted_iota(jnp.int32, (top, spare), 0)
    lane = lax.broadcasted_iota(jnp.int32, (top, spare), 1)
    turn = (((0,), (0,)), ((), ()))
    tail = lax.dot_general(
        ids_ref[...].astype(f32), jnp.where(lane == sub, 1.0, 0.0), turn, preferred_element_type=f32
    ) + lax.dot_general(
        gates_ref[...].astype(f32), jnp.where(lane == sub + top, 1.0, 0.0), turn, preferred_element_type=f32
    )
    at = 0
    for ref in out_refs:
        end = at + ref.shape[1]
        ref[:, : min(end, width) - at] = normed[:, at : min(end, width)]
        if end > width:
            ref[:, width - at :] = tail.astype(bf16)
        at = end


def pick_kernel(top, width, counts, experts_ref, *refs):
    f32, bf16 = jnp.float32, jnp.bfloat16
    pieces, (own_out, mate_out, placer_out, held) = refs[: sum(counts)], refs[sum(counts) :]
    at_piece = lane_at = 0
    for count in counts:
        row_at = 0
        for ref in pieces[at_piece : at_piece + count]:
            rows, lanes = ref.shape
            held[row_at : row_at + rows, lane_at : lane_at + lanes] = ref[...]
            row_at += rows
        at_piece, lane_at = at_piece + count, lane_at + lanes
    tail = held[:, width:]
    slots = own_out.shape[0]
    rows = tail.shape[0]
    sub = lax.broadcasted_iota(jnp.int32, (16, tail.shape[1]), 0)
    lane = lax.broadcasted_iota(jnp.int32, (16, tail.shape[1]), 1)
    pick_id = jnp.where((sub == lane) & (sub < top), 1.0, 0.0).astype(bf16)
    ids = lax.dot_general(pick_id, tail, (((1,), (1,)), ((), ())), preferred_element_type=f32)
    entry = lax.broadcasted_iota(jnp.int32, ids.shape, 0)
    first = lax.broadcasted_iota(jnp.int32, (rows, rows), 0)
    second = lax.broadcasted_iota(jnp.int32, (rows, rows), 1)
    upper = jnp.where(first <= second, 1.0, 0.0).astype(bf16)
    lower = jnp.where(first >= second, 1.0, 0.0).astype(bf16)
    tail_float = tail.astype(f32)
    tail_lane = lax.broadcasted_iota(jnp.int32, tail.shape, 1)
    slot = lax.broadcasted_iota(jnp.int32, (slots, rows), 0).astype(f32) + 1.0
    slot_lane = lax.broadcasted_iota(jnp.int32, (rows, slots), 1).astype(f32) + 1.0
    placers = []
    for i, out in enumerate((own_out, mate_out)):
        expert = experts_ref[0, i].astype(f32)
        named = jnp.sum(jnp.where((ids == expert) & (entry < top), 1.0, 0.0), axis=0, keepdims=True)
        count = jnp.dot(jnp.broadcast_to(named, (16, rows)).astype(bf16), upper, preferred_element_type=f32)[:1]
        picker = jnp.where((count == slot) & (named > 0.5), 1.0, 0.0).astype(bf16)
        out[...] = jnp.dot(picker, held[...], preferred_element_type=f32).astype(bf16)
        named = jnp.sum(jnp.where((tail_float == expert) & (tail_lane < top), 1.0, 0.0), axis=1, keepdims=True)
        count = jnp.dot(lower, jnp.broadcast_to(named, (rows, LANES)).astype(bf16), preferred_element_type=f32)
        placers.append(jnp.where((count[:, :1] == slot_lane) & (named > 0.5), 1.0, 0.0))
    placer_out[...] = jnp.concatenate(placers, axis=1).astype(bf16)


def slot_weights(rows, width, top, expert):
    f32 = jnp.float32
    tail = rows[:, width:]
    lane = lax.broadcasted_iota(jnp.int32, tail.shape, 1)
    spare = tail.shape[1]
    first = lax.broadcasted_iota(jnp.int32, (spare, spare), 0)
    second = lax.broadcasted_iota(jnp.int32, (spare, spare), 1)
    shift = jnp.where((first == second + top) & (second < top), 1.0, 0.0).astype(jnp.bfloat16)
    gates = jnp.dot(tail, shift, preferred_element_type=f32)
    hit = (tail.astype(f32) == expert) & (lane < top)
    total = jnp.sum(gates, axis=1, keepdims=True)
    return jnp.sum(jnp.where(hit, gates, 0.0), axis=1, keepdims=True) / jnp.maximum(total, 1.0)


def expert_kernel(
    top, steps_in, experts_ref, own_ref, mate_ref, win_ref, bin_ref, wout_ref, bout_ref,
    own_out, mate_out, act_out, weight_out, picked, pre,
):
    step = pl.program_id(0)
    f32, bf16 = jnp.float32, jnp.bfloat16
    slots, hidden, width = own_ref.shape[0], act_out.shape[1], picked.shape[1]

    @pl.when(step == 0)
    def _():
        picked[:slots] = own_ref[:, :width]
        picked[slots:] = mate_ref[:, :width]
        expert = experts_ref[0, 0].astype(f32)
        for i, ref in enumerate((own_ref, mate_ref)):
            weight = slot_weights(ref, width, top, expert)
            weight_out[i * slots : (i + 1) * slots] = jnp.broadcast_to(weight, (slots, LANES))

    @pl.when(step < steps_in)
    def _():
        at = pl.multiple_of(step * BLOCK, BLOCK)
        pre[:, pl.ds(at, BLOCK)] = jnp.dot(picked[...], win_ref[0], preferred_element_type=f32) + bin_ref[...]

    @pl.when(step == steps_in)
    def _():
        for at in range(0, hidden, 256):
            end = min(at + 256, hidden)
            gate = pre[:, at:end]
            up = pre[:, hidden + at : hidden + end]
            act_out[:, at:end] = (gate * jax.nn.sigmoid(1.702 * gate) * (up + 1.0)).astype(bf16)

    @pl.when(step >= steps_in)
    def _():
        result = jnp.dot(act_out[...], wout_ref[0], preferred_element_type=f32) + bout_ref[...]
        result = (result * weight_out[:, :1]).astype(bf16)
        own_out[...] = result[:slots]
        mate_out[...] = result[slots:]


def second_kernel(act_ref, weight_ref, wout_ref, bout_ref, own_out, mate_out):
    slots = own_out.shape[0]
    result = jnp.dot(act_ref[...], wout_ref[0], preferred_element_type=jnp.float32) + bout_ref[...]
    result = (result * weight_ref[:, :1]).astype(jnp.bfloat16)
    own_out[...] = result[:slots]
    mate_out[...] = result[slots:]


def spread_kernel(placer_ref, own_ref, mate_ref, *out_refs):
    slots = own_ref.shape[0]
    f32 = jnp.float32
    at = 0
    for ref in out_refs:
        rows = ref.shape[0]
        part = placer_ref[at : at + rows]
        total = jnp.dot(part[:, :slots], own_ref[...], preferred_element_type=f32)
        total += jnp.dot(part[:, slots:], mate_ref[...], preferred_element_type=f32)
        ref[...] = total.astype(ref.dtype)
        at += rows


def params(mib):
    return pltpu.CompilerParams(vmem_limit_bytes=mib * 2**20)


def ring_shards(tokens, expert_ids, gate_ints, norm_gain, weight_in, bias_in, weight_out, bias_out):
    device_count = lax.axis_size("ep")
    chips = device_count // 2
    reach = chips // 2
    ring = list(range(0, chips, 2)) + list(range(chips - 1, 0, -2))
    right = [(ring[i] * 2 + k, ring[(i + 1) % chips] * 2 + k) for i in range(chips) for k in range(2)]
    left = [(b, a) for a, b in right]
    mate = [(i, i ^ 1) for i in range(device_count)]
    send = lambda value, pairs: lax.ppermute(value, "ep", pairs)
    bf16, f32 = jnp.bfloat16, jnp.float32
    row_count, width = tokens.shape
    top = expert_ids.shape[1]
    hidden = weight_out.shape[1]
    half = row_count // 2
    wide = width + -width % LANES
    lanes = [2 * BLOCK, wide - 2 * BLOCK]
    slots = chips * CAP
    vmem = pl.BlockSpec(memory_space=pltpu.VMEM)
    smem = pl.BlockSpec(memory_space=pltpu.SMEM)
    shape = lambda rows, cols, dtype=bf16: jax.ShapeDtypeStruct((rows, cols), dtype)

    chains = pl.pallas_call(
        functools.partial(norm_kernel, top),
        in_specs=[vmem] * 4,
        out_specs=[vmem] * 2,
        out_shape=[shape(row_count, w) for w in lanes],
        compiler_params=params(16),
    )(tokens, expert_ids.T, gate_ints.T, norm_gain[None, :])
    me = lax.axis_index("ep").astype(jnp.int32)
    experts = jnp.stack([me, me ^ 1]).reshape(1, 2)
    bias_row = lax.dynamic_slice_in_dim(bias_out, me, 1, axis=0)

    held = [[chain] for chain in chains]
    going = [(chain, chain) for chain in chains]
    for hop in range(1, reach + 1):
        for c in range(len(chains)):
            to_right, to_left = going[c]
            if hop == reach:
                to_right, to_left = to_right[:half], to_left[half:]
            going[c] = send(to_right, right), send(to_left, left)
            held[c] += going[c]
    order = [0]
    for hop in range(1, reach):
        order += [-hop, hop]
    pieces = held[0] + held[1]
    picked, picked_mate, placer = pl.pallas_call(
        functools.partial(pick_kernel, top, width, [len(h) for h in held]),
        in_specs=[smem] + [vmem] * len(pieces),
        out_specs=[vmem] * 3,
        out_shape=[shape(slots, wide), shape(slots, wide), shape(chips * row_count, 2 * slots)],
        scratch_shapes=[pltpu.VMEM((chips * row_count, wide), bf16)],
        compiler_params=params(24),
    )(experts, *pieces)
    picked_mate = send(picked_mate, mate)

    steps_in = pl.cdiv(2 * hidden, BLOCK)
    steps_a = lanes[0] // BLOCK
    steps_b = pl.cdiv(width - lanes[0], BLOCK)
    first = lambda j: jnp.minimum(j, steps_in - 1)
    second = lambda j: jnp.maximum(j - steps_in, 0)
    whole = lambda rows, cols: pl.BlockSpec((rows, cols), lambda j: (0, 0), pipeline_mode=pl.Buffered(1))
    own_a, mate_a, act, slot_weight = pl.pallas_call(
        functools.partial(expert_kernel, top, steps_in),
        grid=(steps_in + steps_a,),
        in_specs=[
            smem, whole(slots, wide), whole(slots, wide),
            pl.BlockSpec((1, width, BLOCK), lambda j: (0, 0, first(j))),
            pl.BlockSpec((1, BLOCK), lambda j: (0, first(j))),
            pl.BlockSpec((1, hidden, BLOCK), lambda j: (0, 0, second(j))),
            pl.BlockSpec((1, BLOCK), lambda j: (0, second(j))),
        ],
        out_specs=[pl.BlockSpec((slots, BLOCK), lambda j: (0, second(j)))] * 2
        + [whole(2 * slots, hidden), whole(2 * slots, LANES)],
        out_shape=[shape(slots, lanes[0])] * 2 + [shape(2 * slots, hidden), shape(2 * slots, LANES, f32)],
        scratch_shapes=[
            pltpu.VMEM((2 * slots, width), bf16),
            pltpu.VMEM((2 * slots, steps_in * BLOCK), f32),
        ],
        compiler_params=params(40),
    )(experts, picked, picked_mate, weight_in, bias_in, weight_out, bias_row)
    own_b, mate_b = pl.pallas_call(
        second_kernel,
        grid=(steps_b,),
        in_specs=[
            whole(2 * slots, hidden), whole(2 * slots, LANES),
            pl.BlockSpec((1, hidden, BLOCK), lambda j: (0, 0, j + steps_a)),
            pl.BlockSpec((1, BLOCK), lambda j: (0, j + steps_a)),
        ],
        out_specs=[pl.BlockSpec((slots, BLOCK), lambda j: (0, j))] * 2,
        out_shape=[shape(slots, lanes[1])] * 2,
        compiler_params=params(24),
    )(act, slot_weight, weight_out, bias_row)

    heights = [row_count] * (chips - 1) + [half, half]
    add = lambda a, b: (a.astype(f32) + b.astype(f32)).astype(bf16)
    owed = []
    for own, other in ((own_a, mate_a), (own_b, mate_b)):
        sums = pl.pallas_call(
            spread_kernel,
            in_specs=[vmem] * 3,
            out_specs=[vmem] * len(heights),
            out_shape=[shape(rows, own.shape[1]) for rows in heights],
            compiler_params=params(16),
        )(placer, own, send(other, mate))
        owed.append(dict(zip(order + ["right", "left"], sums)))
    going = [(o["right"], o["left"]) for o in owed]
    for hop in range(reach - 1, -1, -1):
        for c in range(len(owed)):
            up, down = send(going[c][0], right), send(going[c][1], left)
            if hop == reach - 1:
                ahead, behind = owed[c][hop], owed[c][-hop]
                up = jnp.concatenate([add(ahead[:half], up), ahead[half:]], axis=0)
                down = jnp.concatenate([behind[:half], add(behind[half:], down)], axis=0)
            elif hop:
                up, down = add(owed[c][hop], up), add(owed[c][-hop], down)
            going[c] = up, down
    moe = [o[0].astype(f32) + up.astype(f32) + down.astype(f32) for o, (up, down) in zip(owed, going)]
    return (tokens.astype(f32) + jnp.concatenate(moe, axis=1)[:, :width]).astype(bf16)


def solution(mesh):
    ep = mesh.shape["ep"]

    def shards(*arrays):
        whole_experts = arrays[-1].shape[0] == ep and ep == 16
        return (ring_shards if whole_experts else exchange_shards)(*arrays)

    return jax.shard_map(
        shards,
        mesh=mesh,
        in_specs=(
            P(("groups", "ep"), None),
            P(("groups", "ep"), None),
            P(("groups", "ep"), None),
            P(),
            P("ep", None, None),
            P("ep", None),
            P("ep", None, None),
            P(),
        ),
        out_specs=P(("groups", "ep"), None),
        check_vma=False,
    )
```

time: 164 us -> 122 us (0.74)
  the two profiles are of different devices: /device:TPU:11 before, /device:TPU:0 now
where the time goes in v2:
time: 122 us; the launch traced here: 121 us
  waiting for transfers between devices  36.6 us (30%)
  starting transfers between devices  35.7 us (29%)
  Pallas kernels  34.1 us (28%)
  local copies, waits for them, and re-layouts  13.2 us (11%)
  other arithmetic  1.58 us (1%)
    ppermute x35, waiting for transfers between devices, ring_shards(): send = lambda value, pairs: lax.ppermute(value, 'ep', pairs)  36.6 us
    ppermute x35, starting transfers between devices, ring_shards(): send = lambda value, pairs: lax.ppermute(value, 'ep', pairs)  35.7 us
    pallas_call x1, Pallas kernels, ring_shards(): pl.pallas_call(functools.partial(expert_kernel, top, steps_in), grid=(ste...  24 us
    unnamed x28, local copies, waits for them, and re-layouts  12.3 us
    pallas_call x1, Pallas kernels, ring_shards(): pl.pallas_call(second_kernel, grid=(steps_b,), in_specs=[whole(2 * slots,...  4.13 us
    pallas_call x1, Pallas kernels, ring_shards(): pl.pallas_call(functools.partial(pick_kernel, top, width, [len(h) for h i...  3.19 us
    pallas_call x2, Pallas kernels, ring_shards(): pl.pallas_call(spread_kernel, in_specs=[vmem] * 3, out_specs=[vmem] * len...  2.48 us
  transfers between devices with their start and end apart: 35, of which 20 were waited for; matrix products, arithmetic and copies ran while one was open for 1% of the time, Pallas kernels for 2%

profile of v2, /device:TPU:0, one launch (start us, length us, event | category | flops | bytes accessed | tf_op | source)
XLA Modules:
  0.0 121.4 jit_solution(11051352732483563489)
XLA Ops:
  3.4 3.1 %collective-permute-start = (bf16[64,1536]{1,0:T(8,128)(2,1)S(1)}, bf16[64,1536]{1,0:T(8,128)(2,1)S(1)}, u32[]{:S(2)}, u32[]{:S(2)}) collective-permute-start(bf16[64,1536]{1,0:T(8,128)(2,1)S(1)} %get-tuple-element.34.refs_0_), channel_id=1, source_target_pairs={{0,4},{1,5},{4,8},{5,9},{8,12},{9,13},{12,14},{13,15},{14,10},{15,... | collective-permute-start | bytes 589832 | tf_op jit(solution)/shard_map/ppermute | solution.py:220
  6.5 2.0 %collective-permute-start.8 = (bf16[64,1408]{1,0:T(8,128)(2,1)S(1)}, bf16[64,1408]{1,0:T(8,128)(2,1)S(1)}, u32[]{:S(2)}, u32[]{:S(2)}) collective-permute-start(bf16[64,1408]{1,0:T(8,128)(2,1)S(1)} %get-tuple-element.35.refs_9_), channel_id=1, source_target_pairs={{0,4},{1,5},{4,8},{5,9},{8,12},{9,13},{12,14},{13,15},{14,10},{15,... | collective-permute-start | bytes 540680 | tf_op jit(solution)/shard_map/ppermute | solution.py:220
  8.5 3.6 %collective-permute-done.refs_1_ = bf16[64,1536]{1,0:T(8,128)(2,1)S(1)} collective-permute-done((bf16[64,1536]{1,0:T(8,128)(2,1)S(1)}, bf16[64,1536]{1,0:T(8,128)(2,1)S(1)}, u32[]{:S(2)}, u32[]{:S(2)}) %collective-permute-start) | collective-permute-done | bytes 196640 | tf_op jit(solution)/shard_map/ppermute | solution.py:220
  12.1 2.1 %collective-permute-start.2 = (bf16[64,1536]{1,0:T(8,128)(2,1)S(1)}, bf16[64,1536]{1,0:T(8,128)(2,1)S(1)}, u32[]{:S(2)}, u32[]{:S(2)}) collective-permute-start(bf16[64,1536]{1,0:T(8,128)(2,1)S(1)} %collective-permute-done.refs_1_), channel_id=1, source_target_pairs={{0,4},{1,5},{4,8},{5,9},{8,12},{9,13},{12,14},{13,15},{14,10},{15,... | collective-permute-start | bytes 589832 | tf_op jit(solution)/shard_map/ppermute | solution.py:220
  14.3 1.7 %collective-permute-done.8.refs_10_ = bf16[64,1408]{1,0:T(8,128)(2,1)S(1)} collective-permute-done((bf16[64,1408]{1,0:T(8,128)(2,1)S(1)}, bf16[64,1408]{1,0:T(8,128)(2,1)S(1)}, u32[]{:S(2)}, u32[]{:S(2)}) %collective-permute-start.8) | collective-permute-done | bytes 180256 | tf_op jit(solution)/shard_map/ppermute | solution.py:220
  16.0 2.1 %collective-permute-start.10 = (bf16[64,1408]{1,0:T(8,128)(2,1)S(1)}, bf16[64,1408]{1,0:T(8,128)(2,1)S(1)}, u32[]{:S(2)}, u32[]{:S(2)}) collective-permute-start(bf16[64,1408]{1,0:T(8,128)(2,1)S(1)} %collective-permute-done.8.refs_10_), channel_id=1, source_target_pairs={{0,4},{1,5},{4,8},{5,9},{8,12},{9,13},{12,14},{13,15},{14,10},{15,... | collective-permute-start | bytes 540680 | tf_op jit(solution)/shard_map/ppermute | solution.py:220
  20.2 2.1 %collective-permute-start.4 = (bf16[64,1536]{1,0:T(8,128)(2,1)S(1)}, bf16[64,1536]{1,0:T(8,128)(2,1)S(1)}, u32[]{:S(2)}, u32[]{:S(2)}) collective-permute-start(bf16[64,1536]{1,0:T(8,128)(2,1)S(1)} %collective-permute-done.2.refs_3_), channel_id=1, source_target_pairs={{0,4},{1,5},{4,8},{5,9},{8,12},{9,13},{12,14},{13,15},{14,10},{15,... | collective-permute-start | bytes 589832 | tf_op jit(solution)/shard_map/ppermute | solution.py:220
  22.4 1.7 %collective-permute-done.10.refs_12_ = bf16[64,1408]{1,0:T(8,128)(2,1)S(1)} collective-permute-done((bf16[64,1408]{1,0:T(8,128)(2,1)S(1)}, bf16[64,1408]{1,0:T(8,128)(2,1)S(1)}, u32[]{:S(2)}, u32[]{:S(2)}) %collective-permute-start.10) | collective-permute-done | bytes 180256 | tf_op jit(solution)/shard_map/ppermute | solution.py:220
  24.1 2.1 %collective-permute-start.12 = (bf16[64,1408]{1,0:T(8,128)(2,1)S(1)}, bf16[64,1408]{1,0:T(8,128)(2,1)S(1)}, u32[]{:S(2)}, u32[]{:S(2)}) collective-permute-start(bf16[64,1408]{1,0:T(8,128)(2,1)S(1)} %collective-permute-done.10.refs_12_), channel_id=1, source_target_pairs={{0,4},{1,5},{4,8},{5,9},{8,12},{9,13},{12,14},{13,15},{14,10},{15,... | collective-permute-start | bytes 540680 | tf_op jit(solution)/shard_map/ppermute | solution.py:220
  26.3 5.1 %collective-permute-done.12.refs_14_ = bf16[64,1408]{1,0:T(8,128)(2,1)S(1)} collective-permute-done((bf16[64,1408]{1,0:T(8,128)(2,1)S(1)}, bf16[64,1408]{1,0:T(8,128)(2,1)S(1)}, u32[]{:S(2)}, u32[]{:S(2)}) %collective-permute-start.12) | collective-permute-done | bytes 180256 | tf_op jit(solution)/shard_map/ppermute | solution.py:220
  31.3 1.9 %collective-permute-start.14 = (bf16[32,1408]{1,0:T(8,128)(2,1)S(1)}, bf16[32,1408]{1,0:T(8,128)(2,1)S(1)}, u32[]{:S(2)}, u32[]{:S(2)}) collective-permute-start(bf16[32,1408]{1,0:T(8,128)(2,1)S(1)} %slice.54), channel_id=1, source_target_pairs={{0,4},{1,5},{4,8},{5,9},{8,12},{9,13},{12,14},{13,15},{14,10},{15,... | collective-permute-start | bytes 270344 | tf_op jit(solution)/shard_map/ppermute | solution.py:220
  33.5 1.9 %collective-permute-start.6 = (bf16[32,1536]{1,0:T(8,128)(2,1)S(1)}, bf16[32,1536]{1,0:T(8,128)(2,1)S(1)}, u32[]{:S(2)}, u32[]{:S(2)}) collective-permute-start(bf16[32,1536]{1,0:T(8,128)(2,1)S(1)} %slice.52), channel_id=1, source_target_pairs={{0,4},{1,5},{4,8},{5,9},{8,12},{9,13},{12,14},{13,15},{14,10},{15,... | collective-permute-start | bytes 294920 | tf_op jit(solution)/shard_map/ppermute | solution.py:220
  38.2 1.9 %collective-permute-done.7.refs_8_ = bf16[32,1536]{1,0:T(8,128)(2,1)S(1)} collective-permute-done((bf16[32,1536]{1,0:T(8,128)(2,1)S(1)}, bf16[32,1536]{1,0:T(8,128)(2,1)S(1)}, u32[]{:S(2)}, u32[]{:S(2)}) %collective-permute-start.7) | collective-permute-done | bytes 98336 | tf_op jit(solution)/shard_map/ppermute | solution.py:220
  42.8 3.2 %shard_map.83 = (bf16[144,2944]{1,0:T(8,128)(2,1)S(1)}, bf16[144,2944]{1,0:T(8,128)(2,1)}, bf16[512,288]{1,0:T(8,128)(2,1)S(1)}) custom-call(s32[1,2]{1,0:T(1,128)S(1)} %add_bitcast_fusion.experts_ref, bf16[64,1536]{1,0:T(8,128)(2,1)S(1)} %get-tuple-element.34.refs_0_, bf16[64,1536]{1,0:T(8,128)(2,1)S(1)} %collective-permute-done.refs_1_, ...), custom_call_target="tpu_custom_call" | custom-call | tf_op jit(solution)/shard_map/pallas_call | solution.py:257
  46.0 2.6 %collective-permute-done.16.mate_ref = bf16[144,2944]{1,0:T(8,128)(2,1)S(1)} collective-permute-done((bf16[144,2944]{1,0:T(8,128)(2,1)}, bf16[144,2944]{1,0:T(8,128)(2,1)S(1)}, u32[]{:S(2)}, u32[]{:S(2)}) %collective-permute-start.16) | collective-permute-done | bytes 847904 | tf_op jit(solution)/shard_map/ppermute | solution.py:220
  49.3 24.0 %shard_map.84 = (bf16[144,1536]{1,0:T(8,128)(2,1)S(1)}, bf16[144,1536]{1,0:T(8,128)(2,1)S(1)}, bf16[288,2880]{1,0:T(8,128)(2,1)S(1)}, f32[288,128]{1,0:T(8,128)S(1)}) custom-call(s32[1,2]{1,0:T(1,128)S(1)} %add_bitcast_fusion.experts_ref, bf16[144,2944]{1,0:T(8,128)(2,1)S(1)} %get-tuple-element.37.own_ref, ...), custom_call_target="tpu_custom_call" | custom-call | tf_op jit(solution)/shard_map/pallas_call | solution.py:273
  73.4 5.8 %copy-done.2 = bf16[1,2880,2880]{2,1,0:T(8,128)(2,1)S(1)} copy-done((bf16[1,2880,2880]{2,1,0:T(8,128)(2,1)S(1)}, bf16[1,2880,2880]{2,1,0:T(8,128)(2,1)}, u32[]{:S(2)}) %copy-start.2) | copy-done | bytes 16588824
  79.2 4.1 %shard_map.86 = (bf16[144,1408]{1,0:T(8,128)(2,1)S(1)}, bf16[144,1408]{1,0:T(8,128)(2,1)S(1)}) custom-call(bf16[288,2880]{1,0:T(8,128)(2,1)S(1)} %get-tuple-element.50.act_ref, f32[288,128]{1,0:T(8,128)S(1)} %get-tuple-element.51.weight_ref, bf16[1,2880,2880]{2,1,0:T(8,128)(2,1)S(1)} %copy-done.2, f32[1,2880]{1,0:T(1,128)S(1)} %constant_dynamic-slice_fusion.bout_ref), custom_call_target="tpu_custom_call" | custom-call | tf_op jit(solution)/shard_map/pallas_call | solution.py:292
  86.4 1.6 %collective-permute-start.27 = (bf16[32,1408]{1,0:T(8,128)(2,1)S(1)}, bf16[32,1408]{1,0:T(8,128)(2,1)S(1)}, u32[]{:S(2)}, u32[]{:S(2)}) collective-permute-start(bf16[32,1408]{1,0:T(8,128)(2,1)S(1)} %get-tuple-element.58), channel_id=1, source_target_pairs={{0,4},{1,5},{4,8},{5,9},{8,12},{9,13},{12,14},{13,15},{14,10},{15,... | collective-permute-start | bytes 270344 | tf_op jit(solution)/shard_map/ppermute | solution.py:220
  90.0 1.6 %collective-permute-start.18 = (bf16[32,1536]{1,0:T(8,128)(2,1)S(1)}, bf16[32,1536]{1,0:T(8,128)(2,1)S(1)}, u32[]{:S(2)}, u32[]{:S(2)}) collective-permute-start(bf16[32,1536]{1,0:T(8,128)(2,1)S(1)} %get-tuple-element.45), channel_id=1, source_target_pairs={{0,4},{1,5},{4,8},{5,9},{8,12},{9,13},{12,14},{13,15},{14,10},{15,... | collective-permute-start | bytes 294920 | tf_op jit(solution)/shard_map/ppermute | solution.py:220
  92.2 1.6 %collective-permute-start.28 = (bf16[64,1408]{1,0:T(8,128)(2,1)S(1)}, bf16[64,1408]{1,0:T(8,128)(2,1)S(1)}, u32[]{:S(2)}, u32[]{:S(2)}) collective-permute-start(bf16[64,1408]{1,0:T(8,128)(2,1)S(1)} %pad_maximum_fusion.3), channel_id=1, source_target_pairs={{0,4},{1,5},{4,8},{5,9},{8,12},{9,13},{12,14},{13,15},{14,10},{15,... | collective-permute-start | bytes 540680 | tf_op jit(solution)/shard_map/ppermute | solution.py:220
  95.5 1.6 %collective-permute-start.19 = (bf16[64,1536]{1,0:T(8,128)(2,1)S(1)}, bf16[64,1536]{1,0:T(8,128)(2,1)S(1)}, u32[]{:S(2)}, u32[]{:S(2)}) collective-permute-start(bf16[64,1536]{1,0:T(8,128)(2,1)S(1)} %pad_maximum_fusion.1), channel_id=1, source_target_pairs={{0,4},{1,5},{4,8},{5,9},{8,12},{9,13},{12,14},{13,15},{14,10},{15,... | collective-permute-start | bytes 589832 | tf_op jit(solution)/shard_map/ppermute | solution.py:220
  97.8 1.9 %collective-permute-done.28 = bf16[64,1408]{1,0:T(8,128)(2,1)S(1)} collective-permute-done((bf16[64,1408]{1,0:T(8,128)(2,1)S(1)}, bf16[64,1408]{1,0:T(8,128)(2,1)S(1)}, u32[]{:S(2)}, u32[]{:S(2)}) %collective-permute-start.28) | collective-permute-done | bytes 180256 | tf_op jit(solution)/shard_map/ppermute | solution.py:220
  99.8 1.6 %collective-permute-start.29 = (bf16[64,1408]{1,0:T(8,128)(2,1)S(1)}, bf16[64,1408]{1,0:T(8,128)(2,1)S(1)}, u32[]{:S(2)}, u32[]{:S(2)}) collective-permute-start(bf16[64,1408]{1,0:T(8,128)(2,1)S(1)} %add_convert_fusion.7), channel_id=1, source_target_pairs={{0,4},{1,5},{4,8},{5,9},{8,12},{9,13},{12,14},{13,15},{14,10},{15,... | collective-permute-start | bytes 540680 | tf_op jit(solution)/shard_map/ppermute | solution.py:220
  102.0 2.0 %collective-permute-done.19 = bf16[64,1536]{1,0:T(8,128)(2,1)S(1)} collective-permute-done((bf16[64,1536]{1,0:T(8,128)(2,1)S(1)}, bf16[64,1536]{1,0:T(8,128)(2,1)S(1)}, u32[]{:S(2)}, u32[]{:S(2)}) %collective-permute-start.19) | collective-permute-done | bytes 196640 | tf_op jit(solution)/shard_map/ppermute | solution.py:220
  104.0 1.6 %collective-permute-start.20 = (bf16[64,1536]{1,0:T(8,128)(2,1)S(1)}, bf16[64,1536]{1,0:T(8,128)(2,1)S(1)}, u32[]{:S(2)}, u32[]{:S(2)}) collective-permute-start(bf16[64,1536]{1,0:T(8,128)(2,1)S(1)} %add_convert_fusion.3), channel_id=1, source_target_pairs={{0,4},{1,5},{4,8},{5,9},{8,12},{9,13},{12,14},{13,15},{14,10},{15,... | collective-permute-start | bytes 589832 | tf_op jit(solution)/shard_map/ppermute | solution.py:220
  107.8 1.6 %collective-permute-start.30 = (bf16[64,1408]{1,0:T(8,128)(2,1)S(1)}, bf16[64,1408]{1,0:T(8,128)(2,1)S(1)}, u32[]{:S(2)}, u32[]{:S(2)}) collective-permute-start(bf16[64,1408]{1,0:T(8,128)(2,1)S(1)} %add_convert_fusion.6), channel_id=1, source_target_pairs={{0,4},{1,5},{4,8},{5,9},{8,12},{9,13},{12,14},{13,15},{14,10},{15,... | collective-permute-start | bytes 540680 | tf_op jit(solution)/shard_map/ppermute | solution.py:220
  110.0 2.0 %collective-permute-done.20 = bf16[64,1536]{1,0:T(8,128)(2,1)S(1)} collective-permute-done((bf16[64,1536]{1,0:T(8,128)(2,1)S(1)}, bf16[64,1536]{1,0:T(8,128)(2,1)S(1)}, u32[]{:S(2)}, u32[]{:S(2)}) %collective-permute-start.20) | collective-permute-done | bytes 196640 | tf_op jit(solution)/shard_map/ppermute | solution.py:220
  112.1 1.6 %collective-permute-start.21 = (bf16[64,1536]{1,0:T(8,128)(2,1)S(1)}, bf16[64,1536]{1,0:T(8,128)(2,1)S(1)}, u32[]{:S(2)}, u32[]{:S(2)}) collective-permute-start(bf16[64,1536]{1,0:T(8,128)(2,1)S(1)} %add_convert_fusion.2), channel_id=1, source_target_pairs={{0,4},{1,5},{4,8},{5,9},{8,12},{9,13},{12,14},{13,15},{14,10},{15,... | collective-permute-start | bytes 589832 | tf_op jit(solution)/shard_map/ppermute | solution.py:220
  114.2 1.6 %collective-permute-done.30 = bf16[64,1408]{1,0:T(8,128)(2,1)S(1)} collective-permute-done((bf16[64,1408]{1,0:T(8,128)(2,1)S(1)}, bf16[64,1408]{1,0:T(8,128)(2,1)S(1)}, u32[]{:S(2)}, u32[]{:S(2)}) %collective-permute-start.30) | collective-permute-done | bytes 180256 | tf_op jit(solution)/shard_map/ppermute | solution.py:220
  115.9 1.7 %collective-permute-done.34 = bf16[64,1408]{1,0:T(8,128)(2,1)S(1)} collective-permute-done((bf16[64,1408]{1,0:T(8,128)(2,1)S(1)}, bf16[64,1408]{1,0:T(8,128)(2,1)S(1)}, u32[]{:S(2)}, u32[]{:S(2)}) %collective-permute-start.34) | collective-permute-done | bytes 180256 | tf_op jit(solution)/shard_map/ppermute | solution.py:220
  118.9 1.6 %collective-permute-done.25 = bf16[64,1536]{1,0:T(8,128)(2,1)S(1)} collective-permute-done((bf16[64,1536]{1,0:T(8,128)(2,1)S(1)}, bf16[64,1536]{1,0:T(8,128)(2,1)S(1)}, u32[]{:S(2)}, u32[]{:S(2)}) %collective-permute-start.25) | collective-permute-done | bytes 196640 | tf_op jit(solution)/shard_map/ppermute | solution.py:220
  (102 shorter events, 26.4 us)
Async XLA Ops:
  3.4 8.7 %collective-permute-start = (bf16[64,1536]{1,0:T(8,128)(2,1)S(1)}, bf16[64,1536]{1,0:T(8,128)(2,1)S(1)}, u32[]{:S(2)}, u32[]{:S(2)}) collective-permute-start(bf16[64,1536]{1,0:T(8,128)(2,1)S(1)} %get-tuple-element.34.refs_0_), channel_id=1, source_target_pairs={{0,4},{1,5},{4,8},{5,9},{8,12},{9,13},{12,14},{13,15},{14,10},{15,... | collective-permute-start | bytes 589832 | tf_op jit(solution)/shard_map/ppermute | solution.py:220
  6.5 7.8 %collective-permute-start.1 = (bf16[64,1536]{1,0:T(8,128)(2,1)S(1)}, bf16[64,1536]{1,0:T(8,128)(2,1)S(1)}, u32[]{:S(2)}, u32[]{:S(2)}) collective-permute-start(bf16[64,1536]{1,0:T(8,128)(2,1)S(1)} %get-tuple-element.34.refs_0_), channel_id=1, source_target_pairs={{4,0},{5,1},{8,4},{9,5},{12,8},{13,9},{14,12},{15,13},{10,14},{11,... | collective-permute-start | bytes 589832 | tf_op jit(solution)/shard_map/ppermute | solution.py:220
  6.5 9.5 %collective-permute-start.8 = (bf16[64,1408]{1,0:T(8,128)(2,1)S(1)}, bf16[64,1408]{1,0:T(8,128)(2,1)S(1)}, u32[]{:S(2)}, u32[]{:S(2)}) collective-permute-start(bf16[64,1408]{1,0:T(8,128)(2,1)S(1)} %get-tuple-element.35.refs_9_), channel_id=1, source_target_pairs={{0,4},{1,5},{4,8},{5,9},{8,12},{9,13},{12,14},{13,15},{14,10},{15,... | collective-permute-start | bytes 540680 | tf_op jit(solution)/shard_map/ppermute | solution.py:220
  8.5 9.7 %collective-permute-start.9 = (bf16[64,1408]{1,0:T(8,128)(2,1)S(1)}, bf16[64,1408]{1,0:T(8,128)(2,1)S(1)}, u32[]{:S(2)}, u32[]{:S(2)}) collective-permute-start(bf16[64,1408]{1,0:T(8,128)(2,1)S(1)} %get-tuple-element.35.refs_9_), channel_id=1, source_target_pairs={{4,0},{5,1},{8,4},{9,5},{12,8},{13,9},{14,12},{15,13},{10,14},{11,... | collective-permute-start | bytes 540680 | tf_op jit(solution)/shard_map/ppermute | solution.py:220
  12.1 8.1 %collective-permute-start.2 = (bf16[64,1536]{1,0:T(8,128)(2,1)S(1)}, bf16[64,1536]{1,0:T(8,128)(2,1)S(1)}, u32[]{:S(2)}, u32[]{:S(2)}) collective-permute-start(bf16[64,1536]{1,0:T(8,128)(2,1)S(1)} %collective-permute-done.refs_1_), channel_id=1, source_target_pairs={{0,4},{1,5},{4,8},{5,9},{8,12},{9,13},{12,14},{13,15},{14,10},{15,... | collective-permute-start | bytes 589832 | tf_op jit(solution)/shard_map/ppermute | solution.py:220
  14.3 8.1 %collective-permute-start.3 = (bf16[64,1536]{1,0:T(8,128)(2,1)S(1)}, bf16[64,1536]{1,0:T(8,128)(2,1)S(1)}, u32[]{:S(2)}, u32[]{:S(2)}) collective-permute-start(bf16[64,1536]{1,0:T(8,128)(2,1)S(1)} %collective-permute-done.1.refs_2_), channel_id=1, source_target_pairs={{4,0},{5,1},{8,4},{9,5},{12,8},{13,9},{14,12},{15,13},{10,14},{11,... | collective-permute-start | bytes 589832 | tf_op jit(solution)/shard_map/ppermute | solution.py:220
  16.0 8.1 %collective-permute-start.10 = (bf16[64,1408]{1,0:T(8,128)(2,1)S(1)}, bf16[64,1408]{1,0:T(8,128)(2,1)S(1)}, u32[]{:S(2)}, u32[]{:S(2)}) collective-permute-start(bf16[64,1408]{1,0:T(8,128)(2,1)S(1)} %collective-permute-done.8.refs_10_), channel_id=1, source_target_pairs={{0,4},{1,5},{4,8},{5,9},{8,12},{9,13},{12,14},{13,15},{14,10},{15,... | collective-permute-start | bytes 540680 | tf_op jit(solution)/shard_map/ppermute | solution.py:220
  18.2 8.1 %collective-permute-start.11 = (bf16[64,1408]{1,0:T(8,128)(2,1)S(1)}, bf16[64,1408]{1,0:T(8,128)(2,1)S(1)}, u32[]{:S(2)}, u32[]{:S(2)}) collective-permute-start(bf16[64,1408]{1,0:T(8,128)(2,1)S(1)} %collective-permute-done.9.refs_11_), channel_id=1, source_target_pairs={{4,0},{5,1},{8,4},{9,5},{12,8},{13,9},{14,12},{15,13},{10,14},{11,... | collective-permute-start | bytes 540680 | tf_op jit(solution)/shard_map/ppermute | solution.py:220
  20.2 13.3 %collective-permute-start.4 = (bf16[64,1536]{1,0:T(8,128)(2,1)S(1)}, bf16[64,1536]{1,0:T(8,128)(2,1)S(1)}, u32[]{:S(2)}, u32[]{:S(2)}) collective-permute-start(bf16[64,1536]{1,0:T(8,128)(2,1)S(1)} %collective-permute-done.2.refs_3_), channel_id=1, source_target_pairs={{0,4},{1,5},{4,8},{5,9},{8,12},{9,13},{12,14},{13,15},{14,10},{15,... | collective-permute-start | bytes 589832 | tf_op jit(solution)/shard_map/ppermute | solution.py:220
  22.4 13.0 %collective-permute-start.5 = (bf16[64,1536]{1,0:T(8,128)(2,1)S(1)}, bf16[64,1536]{1,0:T(8,128)(2,1)S(1)}, u32[]{:S(2)}, u32[]{:S(2)}) collective-permute-start(bf16[64,1536]{1,0:T(8,128)(2,1)S(1)} %collective-permute-done.3.refs_4_), channel_id=1, source_target_pairs={{4,0},{5,1},{8,4},{9,5},{12,8},{13,9},{14,12},{15,13},{10,14},{11,... | collective-permute-start | bytes 589832 | tf_op jit(solution)/shard_map/ppermute | solution.py:220
  24.1 7.2 %collective-permute-start.12 = (bf16[64,1408]{1,0:T(8,128)(2,1)S(1)}, bf16[64,1408]{1,0:T(8,128)(2,1)S(1)}, u32[]{:S(2)}, u32[]{:S(2)}) collective-permute-start(bf16[64,1408]{1,0:T(8,128)(2,1)S(1)} %collective-permute-done.10.refs_12_), channel_id=1, source_target_pairs={{0,4},{1,5},{4,8},{5,9},{8,12},{9,13},{12,14},{13,15},{14,10},{15,... | collective-permute-start | bytes 540680 | tf_op jit(solution)/shard_map/ppermute | solution.py:220
  26.3 7.0 %collective-permute-start.13 = (bf16[64,1408]{1,0:T(8,128)(2,1)S(1)}, bf16[64,1408]{1,0:T(8,128)(2,1)S(1)}, u32[]{:S(2)}, u32[]{:S(2)}) collective-permute-start(bf16[64,1408]{1,0:T(8,128)(2,1)S(1)} %collective-permute-done.11.refs_13_), channel_id=1, source_target_pairs={{4,0},{5,1},{8,4},{9,5},{12,8},{13,9},{14,12},{15,13},{10,14},{11,... | collective-permute-start | bytes 540680 | tf_op jit(solution)/shard_map/ppermute | solution.py:220
  31.3 5.5 %collective-permute-start.14 = (bf16[32,1408]{1,0:T(8,128)(2,1)S(1)}, bf16[32,1408]{1,0:T(8,128)(2,1)S(1)}, u32[]{:S(2)}, u32[]{:S(2)}) collective-permute-start(bf16[32,1408]{1,0:T(8,128)(2,1)S(1)} %slice.54), channel_id=1, source_target_pairs={{0,4},{1,5},{4,8},{5,9},{8,12},{9,13},{12,14},{13,15},{14,10},{15,... | collective-permute-start | bytes 270344 | tf_op jit(solution)/shard_map/ppermute | solution.py:220
  33.2 4.9 %collective-permute-start.15 = (bf16[32,1408]{1,0:T(8,128)(2,1)S(1)}, bf16[32,1408]{1,0:T(8,128)(2,1)S(1)}, u32[]{:S(2)}, u32[]{:S(2)}) collective-permute-start(bf16[32,1408]{1,0:T(8,128)(2,1)S(1)} %slice.55), channel_id=1, source_target_pairs={{4,0},{5,1},{8,4},{9,5},{12,8},{13,9},{14,12},{15,13},{10,14},{11,... | collective-permute-start | bytes 270344 | tf_op jit(solution)/shard_map/ppermute | solution.py:220
  33.5 4.7 %collective-permute-start.6 = (bf16[32,1536]{1,0:T(8,128)(2,1)S(1)}, bf16[32,1536]{1,0:T(8,128)(2,1)S(1)}, u32[]{:S(2)}, u32[]{:S(2)}) collective-permute-start(bf16[32,1536]{1,0:T(8,128)(2,1)S(1)} %slice.52), channel_id=1, source_target_pairs={{0,4},{1,5},{4,8},{5,9},{8,12},{9,13},{12,14},{13,15},{14,10},{15,... | collective-permute-start | bytes 294920 | tf_op jit(solution)/shard_map/ppermute | solution.py:220
  83.6 5.2 %collective-permute-start.17 = (bf16[144,1536]{1,0:T(8,128)(2,1)S(1)}, bf16[144,1536]{1,0:T(8,128)(2,1)S(1)}, u32[]{:S(2)}, u32[]{:S(2)}) collective-permute-start(bf16[144,1536]{1,0:T(8,128)(2,1)S(1)} %get-tuple-element.40), channel_id=1, source_target_pairs={{0,1},{1,0},{2,3},{3,2},{4,5},{5,4},{6,7},{7,6},{8,9},{9,8},{10,11... | collective-permute-start | bytes 1327112 | tf_op jit(solution)/shard_map/ppermute | solution.py:220
  86.4 5.7 %collective-permute-start.27 = (bf16[32,1408]{1,0:T(8,128)(2,1)S(1)}, bf16[32,1408]{1,0:T(8,128)(2,1)S(1)}, u32[]{:S(2)}, u32[]{:S(2)}) collective-permute-start(bf16[32,1408]{1,0:T(8,128)(2,1)S(1)} %get-tuple-element.58), channel_id=1, source_target_pairs={{0,4},{1,5},{4,8},{5,9},{8,12},{9,13},{12,14},{13,15},{14,10},{15,... | collective-permute-start | bytes 270344 | tf_op jit(solution)/shard_map/ppermute | solution.py:220
  88.0 5.8 %collective-permute-start.31 = (bf16[32,1408]{1,0:T(8,128)(2,1)S(1)}, bf16[32,1408]{1,0:T(8,128)(2,1)S(1)}, u32[]{:S(2)}, u32[]{:S(2)}) collective-permute-start(bf16[32,1408]{1,0:T(8,128)(2,1)S(1)} %get-tuple-element.62), channel_id=1, source_target_pairs={{4,0},{5,1},{8,4},{9,5},{12,8},{13,9},{14,12},{15,13},{10,14},{11,... | collective-permute-start | bytes 270344 | tf_op jit(solution)/shard_map/ppermute | solution.py:220
  90.0 5.5 %collective-permute-start.18 = (bf16[32,1536]{1,0:T(8,128)(2,1)S(1)}, bf16[32,1536]{1,0:T(8,128)(2,1)S(1)}, u32[]{:S(2)}, u32[]{:S(2)}) collective-permute-start(bf16[32,1536]{1,0:T(8,128)(2,1)S(1)} %get-tuple-element.45), channel_id=1, source_target_pairs={{0,4},{1,5},{4,8},{5,9},{8,12},{9,13},{12,14},{13,15},{14,10},{15,... | collective-permute-start | bytes 294920 | tf_op jit(solution)/shard_map/ppermute | solution.py:220
  91.6 5.7 %collective-permute-start.22 = (bf16[32,1536]{1,0:T(8,128)(2,1)S(1)}, bf16[32,1536]{1,0:T(8,128)(2,1)S(1)}, u32[]{:S(2)}, u32[]{:S(2)}) collective-permute-start(bf16[32,1536]{1,0:T(8,128)(2,1)S(1)} %get-tuple-element.49), channel_id=1, source_target_pairs={{4,0},{5,1},{8,4},{9,5},{12,8},{13,9},{14,12},{15,13},{10,14},{11,... | collective-permute-start | bytes 294920 | tf_op jit(solution)/shard_map/ppermute | solution.py:220
  92.2 7.5 %collective-permute-start.28 = (bf16[64,1408]{1,0:T(8,128)(2,1)S(1)}, bf16[64,1408]{1,0:T(8,128)(2,1)S(1)}, u32[]{:S(2)}, u32[]{:S(2)}) collective-permute-start(bf16[64,1408]{1,0:T(8,128)(2,1)S(1)} %pad_maximum_fusion.3), channel_id=1, source_target_pairs={{0,4},{1,5},{4,8},{5,9},{8,12},{9,13},{12,14},{13,15},{14,10},{15,... | collective-permute-start | bytes 540680 | tf_op jit(solution)/shard_map/ppermute | solution.py:220
  93.9 7.5 %collective-permute-start.32 = (bf16[64,1408]{1,0:T(8,128)(2,1)S(1)}, bf16[64,1408]{1,0:T(8,128)(2,1)S(1)}, u32[]{:S(2)}, u32[]{:S(2)}) collective-permute-start(bf16[64,1408]{1,0:T(8,128)(2,1)S(1)} %pad_maximum_fusion.4), channel_id=1, source_target_pairs={{4,0},{5,1},{8,4},{9,5},{12,8},{13,9},{14,12},{15,13},{10,14},{11,... | collective-permute-start | bytes 540680 | tf_op jit(solution)/shard_map/ppermute | solution.py:220
  95.5 8.4 %collective-permute-start.19 = (bf16[64,1536]{1,0:T(8,128)(2,1)S(1)}, bf16[64,1536]{1,0:T(8,128)(2,1)S(1)}, u32[]{:S(2)}, u32[]{:S(2)}) collective-permute-start(bf16[64,1536]{1,0:T(8,128)(2,1)S(1)} %pad_maximum_fusion.1), channel_id=1, source_target_pairs={{0,4},{1,5},{4,8},{5,9},{8,12},{9,13},{12,14},{13,15},{14,10},{15,... | collective-permute-start | bytes 589832 | tf_op jit(solution)/shard_map/ppermute | solution.py:220
  97.3 8.3 %collective-permute-start.23 = (bf16[64,1536]{1,0:T(8,128)(2,1)S(1)}, bf16[64,1536]{1,0:T(8,128)(2,1)S(1)}, u32[]{:S(2)}, u32[]{:S(2)}) collective-permute-start(bf16[64,1536]{1,0:T(8,128)(2,1)S(1)} %pad_maximum_fusion.2), channel_id=1, source_target_pairs={{4,0},{5,1},{8,4},{9,5},{12,8},{13,9},{14,12},{15,13},{10,14},{11,... | collective-permute-start | bytes 589832 | tf_op jit(solution)/shard_map/ppermute | solution.py:220
  99.8 8.0 %collective-permute-start.29 = (bf16[64,1408]{1,0:T(8,128)(2,1)S(1)}, bf16[64,1408]{1,0:T(8,128)(2,1)S(1)}, u32[]{:S(2)}, u32[]{:S(2)}) collective-permute-start(bf16[64,1408]{1,0:T(8,128)(2,1)S(1)} %add_convert_fusion.7), channel_id=1, source_target_pairs={{0,4},{1,5},{4,8},{5,9},{8,12},{9,13},{12,14},{13,15},{14,10},{15,... | collective-permute-start | bytes 540680 | tf_op jit(solution)/shard_map/ppermute | solution.py:220
  101.5 8.0 %collective-permute-start.33 = (bf16[64,1408]{1,0:T(8,128)(2,1)S(1)}, bf16[64,1408]{1,0:T(8,128)(2,1)S(1)}, u32[]{:S(2)}, u32[]{:S(2)}) collective-permute-start(bf16[64,1408]{1,0:T(8,128)(2,1)S(1)} %add_convert_fusion.5), channel_id=1, source_target_pairs={{4,0},{5,1},{8,4},{9,5},{12,8},{13,9},{14,12},{15,13},{10,14},{11,... | collective-permute-start | bytes 540680 | tf_op jit(solution)/shard_map/ppermute | solution.py:220
  104.0 8.0 %collective-permute-start.20 = (bf16[64,1536]{1,0:T(8,128)(2,1)S(1)}, bf16[64,1536]{1,0:T(8,128)(2,1)S(1)}, u32[]{:S(2)}, u32[]{:S(2)}) collective-permute-start(bf16[64,1536]{1,0:T(8,128)(2,1)S(1)} %add_convert_fusion.3), channel_id=1, source_target_pairs={{0,4},{1,5},{4,8},{5,9},{8,12},{9,13},{12,14},{13,15},{14,10},{15,... | collective-permute-start | bytes 589832 | tf_op jit(solution)/shard_map/ppermute | solution.py:220
  105.7 8.0 %collective-permute-start.24 = (bf16[64,1536]{1,0:T(8,128)(2,1)S(1)}, bf16[64,1536]{1,0:T(8,128)(2,1)S(1)}, u32[]{:S(2)}, u32[]{:S(2)}) collective-permute-start(bf16[64,1536]{1,0:T(8,128)(2,1)S(1)} %add_convert_fusion.1), channel_id=1, source_target_pairs={{4,0},{5,1},{8,4},{9,5},{12,8},{13,9},{14,12},{15,13},{10,14},{11,... | collective-permute-start | bytes 589832 | tf_op jit(solution)/shard_map/ppermute | solution.py:220
  107.8 8.0 %collective-permute-start.30 = (bf16[64,1408]{1,0:T(8,128)(2,1)S(1)}, bf16[64,1408]{1,0:T(8,128)(2,1)S(1)}, u32[]{:S(2)}, u32[]{:S(2)}) collective-permute-start(bf16[64,1408]{1,0:T(8,128)(2,1)S(1)} %add_convert_fusion.6), channel_id=1, source_target_pairs={{0,4},{1,5},{4,8},{5,9},{8,12},{9,13},{12,14},{13,15},{14,10},{15,... | collective-permute-start | bytes 540680 | tf_op jit(solution)/shard_map/ppermute | solution.py:220
  109.5 8.0 %collective-permute-start.34 = (bf16[64,1408]{1,0:T(8,128)(2,1)S(1)}, bf16[64,1408]{1,0:T(8,128)(2,1)S(1)}, u32[]{:S(2)}, u32[]{:S(2)}) collective-permute-start(bf16[64,1408]{1,0:T(8,128)(2,1)S(1)} %add_convert_fusion.4), channel_id=1, source_target_pairs={{4,0},{5,1},{8,4},{9,5},{12,8},{13,9},{14,12},{15,13},{10,14},{11,... | collective-permute-start | bytes 540680 | tf_op jit(solution)/shard_map/ppermute | solution.py:220
  112.1 6.8 %collective-permute-start.21 = (bf16[64,1536]{1,0:T(8,128)(2,1)S(1)}, bf16[64,1536]{1,0:T(8,128)(2,1)S(1)}, u32[]{:S(2)}, u32[]{:S(2)}) collective-permute-start(bf16[64,1536]{1,0:T(8,128)(2,1)S(1)} %add_convert_fusion.2), channel_id=1, source_target_pairs={{0,4},{1,5},{4,8},{5,9},{8,12},{9,13},{12,14},{13,15},{14,10},{15,... | collective-permute-start | bytes 589832 | tf_op jit(solution)/shard_map/ppermute | solution.py:220
  113.7 6.8 %collective-permute-start.25 = (bf16[64,1536]{1,0:T(8,128)(2,1)S(1)}, bf16[64,1536]{1,0:T(8,128)(2,1)S(1)}, u32[]{:S(2)}, u32[]{:S(2)}) collective-permute-start(bf16[64,1536]{1,0:T(8,128)(2,1)S(1)} %add_convert_fusion), channel_id=1, source_target_pairs={{4,0},{5,1},{8,4},{9,5},{12,8},{13,9},{14,12},{15,13},{10,14},{11,... | collective-permute-start | bytes 589832 | tf_op jit(solution)/shard_map/ppermute | solution.py:220
  (17 other events, 236.8 us)
